TPU v7x, 256 devices: a whole 4x4x8 slice. The times are simulated.
256 devices in a mesh: rows: 32 (over z, y), days: 8 (over x, core).
Axes of the slice: x: 4, y: 4, z: 8, core: 2. Of those that a mesh axis runs over, the one named last changes fastest.
Arguments:
- observations: float32 [256, 128, 1024], P('days', 'rows'), may hold values from -12 to 12, as said below
- obs_mask: int32 [256, 128, 1024], P('days', 'rows'), may hold values 0 or 1
- obs_weight: float32 [128, 1024], P('rows'), may hold values from 0.5 to 4
- classes: int32 [128, 1024], P('rows'), may hold values from 0 to 15
- kappa_table: float32 [16], replicated, may hold values from 0.02 to 2
Outputs:
- solution: float32 [256, 128, 1024], P('days', 'rows')
- residual: float32 [256, 128, 1024], P('days', 'rows')
Inputs may be any that keep to these rules, and one draw needn't show every extreme that they name: `observations`: observed values, given at every cell and day whether observed or not.
All inputs are finite; a program needn't handle non-finite values. No bound on the sum of `obs_mask` on one device may be relied on, other than what follows from the above.
Results may differ from a plain program's by a relative error of at most 0.0003.
Values sent between devices are 32-bit elements; how exact they have to be, the bound alone decides.
A program may use at most 64 MiB of HBM per device.

v0:
```python
import jax
import jax.numpy as jnp
from jax import lax
from jax.sharding import PartitionSpec as P

DEG = 8
ITERS = 2


TIME_SHIFT = 0.05
HALF_OBS = 0.5
KAPPA_LOW = 0.02
KAPPA_HIGH = 2.0
WEIGHT_LOW = 0.5
WEIGHT_HIGH = 4.0
CENTRE_WEIGHT = 20.0 / 6.0
EDGE_WEIGHT = 4.0 / 6.0
CORNER_WEIGHT = 1.0 / 6.0
STENCIL_TOP = 16.0 / 3.0


def with_halo(array, sides, width):
    for axis, dim in sides:
        peers, length = (lax.axis_size(axis), array.shape[dim])
        up = [(i, (i + 1) % peers) for i in range(peers - 1)]
        down = [(j, i) for i, j in up]
        last = lax.slice_in_dim(array, length - width, length, axis=dim)
        leading = lax.slice_in_dim(array, 0, width, axis=dim)
        before = lax.ppermute(last, axis, up)
        after = lax.ppermute(leading, axis, down)
        array = jnp.concatenate([before, array, after], axis=dim)
    return array


def time_basis(first, count, total):
    moment = jnp.arange(count, dtype=jnp.int32) + first
    orders = jnp.arange(total, dtype=jnp.int32)
    phase = (moment[:, None] + 1) * (orders[None, :] + 1) % (2 * (total + 1))
    return jnp.sqrt(2.0 / (total + 1)) * jnp.sin(jnp.pi * phase.astype(jnp.float32) / (total + 1))


def mode_eigs(first, count, total):
    orders = (jnp.arange(count, dtype=jnp.int32) + first + 1).astype(jnp.float32)
    return 2.0 + TIME_SHIFT - 2.0 * jnp.cos(jnp.pi * orders / (total + 1))


def nine_point(padded, core):
    framed = jnp.pad(padded, ((0, 0), (0, 0), (1, 1)))
    edges = framed[:, :-2, 1:-1] + framed[:, 2:, 1:-1] + framed[:, 1:-1, :-2] + framed[:, 1:-1, 2:]
    corners = framed[:, :-2, :-2] + framed[:, :-2, 2:] + framed[:, 2:, :-2] + framed[:, 2:, 2:]
    return CENTRE_WEIGHT * core - EDGE_WEIGHT * edges - CORNER_WEIGHT * corners


def chebyshev(rhs, eigen_vals, apply_fn):
    lower = eigen_vals * KAPPA_LOW + HALF_OBS * WEIGHT_LOW
    upper = eigen_vals * (KAPPA_HIGH + STENCIL_TOP) + HALF_OBS * WEIGHT_HIGH
    centre = 0.5 * (upper + lower)
    spread = 0.5 * (upper - lower)
    stretch = centre / spread
    ratio = 1.0 / stretch
    result = jnp.zeros_like(rhs)
    remainder = rhs
    update = rhs / centre
    for sweep in range(DEG):
        result = result + update
        if sweep + 1 < DEG:
            remainder = remainder - apply_fn(update)
            ratio_next = 1.0 / (2.0 * stretch - ratio)
            update = ratio_next * ratio * update + 2.0 * ratio_next / spread * remainder
            ratio = ratio_next
    return result


def body(observations, obs_mask, obs_weight, classes, kappa_table):
    days_dev = observations.shape[0]
    total = days_dev * lax.axis_size("days")
    first = lax.axis_index("days") * days_dev
    levels = jnp.arange(kappa_table.shape[0], dtype=jnp.int32)
    kappa_cell = jnp.sum(
        jnp.where(classes[None] == levels[:, None, None], kappa_table[:, None, None], 0.0), axis=0
    )
    seen_weight = obs_mask.astype(jnp.float32) * obs_weight
    rhs = seen_weight * observations
    eigen_vals = mode_eigs(first, days_dev, total)[:, None, None]
    local_basis = time_basis(first, days_dev, total)

    def mode_apply(field):
        padded = with_halo(field, (("rows", 1),), 1)
        return (
            eigen_vals * (kappa_cell * field + nine_point(padded, field))
            + HALF_OBS * obs_weight * field
        )

    def to_modes(field):
        return lax.psum_scatter(
            jnp.einsum("tk,txy->kxy", local_basis, field, precision=lax.Precision.HIGHEST),
            "days",
            scatter_dimension=0,
            tiled=True,
        )

    def from_modes(modes):
        return lax.psum_scatter(
            jnp.einsum("kt,kxy->txy", local_basis, modes, precision=lax.Precision.HIGHEST),
            "days",
            scatter_dimension=0,
            tiled=True,
        )

    def precondition(current):
        return from_modes(chebyshev(to_modes(current), eigen_vals, mode_apply))

    def fit_sum(current, precond):
        return lax.psum(jnp.sum(current * precond), ("rows", "days"))

    solution = jnp.zeros_like(rhs)
    residual = rhs
    precond = precondition(residual)
    direction = precond
    fit = fit_sum(residual, precond)
    for step in range(ITERS):
        day_pad = with_halo(direction, (("days", 0),), 1)
        coupled = (2.0 + TIME_SHIFT) * direction - day_pad[:-2] - day_pad[2:]
        operate_padded = with_halo(coupled, (("rows", 1),), 1)
        image = kappa_cell * coupled + nine_point(operate_padded, coupled) + seen_weight * direction
        alpha = fit / lax.psum(jnp.sum(direction * image), ("rows", "days"))
        solution = solution + alpha * direction
        residual = residual - alpha * image
        if step + 1 < ITERS:
            precond = precondition(residual)
            fit_next = fit_sum(residual, precond)
            direction = precond + fit_next / fit * direction
            fit = fit_next
    return (solution, residual)


def solution(mesh):
    in_specs = (
        P("days", "rows", None),
        P("days", "rows", None),
        P("rows", None),
        P("rows", None),
        P(),
    )
    out_specs = (P("days", "rows", None), P("days", "rows", None))
    return jax.shard_map(body, mesh=mesh, in_specs=in_specs, out_specs=out_specs, check_vma=False)
```

profile of v0, /device:TPU:1, one launch (start us, length us, event | category | flops | bytes accessed | tf_op | source)
XLA Modules:
  0.0 667.7 jit_solution(1328680323914323641)
XLA Ops:
  9.1 5.5 fusion.214
  14.8 41.2 %reduce-scatter.5.cloned.1.call-done = f32[32,4,1024]{2,0,1:T(8,128)} async-done(((f32[256,4,1024]{2,0,1:T(8,128)}), f32[32,4,1024]{2,0,1:T(8,128)}) %reduce-scatter.5.cloned.1.call-update) | async-done | bytes 524304 | tf_op jit(solution)/shard_map/reduce_scatter | solution.py:95
  62.3 3.8 collective-permute-done.1
  73.4 3.8 collective-permute-done.3
  78.0 4.6 collective-permute-start.4
  84.5 3.8 collective-permute-done.5
  94.9 3.8 collective-permute-done.7
  99.5 4.0 collective-permute-start.8
  105.5 3.8 collective-permute-done.9
  110.2 4.0 collective-permute-start.10
  116.1 3.8 collective-permute-done.11
  120.8 4.0 collective-permute-start.12
  127.6 4.1 collective-permute-done.13
  132.1 5.9 fusion.101
  138.0 56.4 %reduce-scatter.7.cloned.1.call-done = f32[32,4,1024]{2,0,1:T(8,128)} async-done(((f32[256,4,1024]{2,0,1:T(8,128)}), f32[32,4,1024]{2,0,1:T(8,128)}) %reduce-scatter.7.cloned.1.call-update) | async-done | bytes 524304 | tf_op jit(solution)/shard_map/reduce_scatter | solution.py:103
  198.5 3.8 collective-permute-start.15
  211.2 3.9 collective-permute-done.17
  217.8 79.9 %all-reduce.16 = (f32[]{:T(128)}, f32[]{:T(128)}) all-reduce(f32[]{:T(128)} %get-tuple-element.7, f32[]{:T(128)} %get-tuple-element.6), channel_id=1, replica_groups=mesh['rows'=32,'days'=8] {'rows','days'}, use_global_device_ids=true, to_apply=%region_4.5 | all-reduce | flops 2 | bytes 16 | tf_op jit(solution)/shard_map/psum | solution.py:114
  299.1 5.5 fusion.211
  304.7 33.9 %reduce-scatter.9.cloned.1.call-done = f32[32,4,1024]{2,0,1:T(8,128)} async-done(((f32[256,4,1024]{2,0,1:T(8,128)}), f32[32,4,1024]{2,0,1:T(8,128)}) %reduce-scatter.9.cloned.1.call-update) | async-done | bytes 524304 | tf_op jit(solution)/shard_map/reduce_scatter | solution.py:95
  360.6 4.6 collective-permute-start.22
  382.1 4.0 collective-permute-start.26
  388.1 3.8 collective-permute-done.27
  392.8 4.0 collective-permute-start.28
  398.7 3.8 collective-permute-done.29
  403.4 4.0 collective-permute-start.30
  410.2 4.1 collective-permute-done.31
  414.6 5.9 fusion.19
  420.6 56.5 %reduce-scatter.11.cloned.1.call-done = f32[32,4,1024]{2,0,1:T(8,128)} async-done(((f32[256,4,1024]{2,0,1:T(8,128)}), f32[32,4,1024]{2,0,1:T(8,128)}) %reduce-scatter.11.cloned.1.call-update) | async-done | bytes 524304 | tf_op jit(solution)/shard_map/reduce_scatter | solution.py:103
  478.9 79.2 %psum.30 = f32[]{:T(128)} all-reduce(f32[]{:T(128)} %multiply_reduce_fusion.1), channel_id=1, replica_groups=mesh['rows'=32,'days'=8] {'rows','days'}, use_global_device_ids=true, to_apply=%region_10.11 | all-reduce | flops 1 | bytes 8 | tf_op jit(solution)/shard_map/psum | solution.py:114
  572.1 4.0 collective-permute-done.35
  577.6 79.8 %psum.31 = f32[]{:T(128)} all-reduce(f32[]{:T(128)} %get-tuple-element.10), channel_id=1, replica_groups=mesh['rows'=32,'days'=8] {'rows','days'}, use_global_device_ids=true, to_apply=%region_12.13 | all-reduce | flops 1 | bytes 8 | tf_op jit(solution)/shard_map/psum | solution.py:126
  (142 shorter events, 115.7 us)
Async XLA Ops:
  7.2 48.9 %reduce-scatter.5.cloned.1.call-start = ((), (), s32[]{:S(2)}) async-start(), calls=%async_computation.4 | async-start | bytes 4718592 | tf_op jit(solution)/shard_map/reduce_scatter | solution.py:95
  14.6 179.9 %reduce-scatter.7.cloned.1.call-start = ((), (), s32[]{:S(2)}) async-start(), calls=%async_computation.5 | async-start | bytes 4718592 | tf_op jit(solution)/shard_map/reduce_scatter | solution.py:103
  60.4 5.7 collective-permute-start.1
  71.4 5.7 collective-permute-start.3
  78.0 6.5 collective-permute-start.4
  82.6 5.7 collective-permute-start.5
  89.2 5.7 collective-permute-start.6
  92.9 5.7 collective-permute-start.7
  99.5 6.0 collective-permute-start.8
  103.6 5.7 collective-permute-start.9
  110.2 6.0 collective-permute-start.10
  114.2 5.7 collective-permute-start.11
  120.8 6.8 %collective-permute-start.12 = (f32[32,1,1024]{2,0,1:T(8,128)S(1)}, f32[32,1,1024]{2,0,1:T(8,128)S(1)}, u32[]{:S(2)}, u32[]{:S(2)}) collective-permute-start(f32[32,1,1024]{2,0,1:T(8,128)S(1)} %get-tuple-element.59), channel_id=1, source_target_pairs={{0,8},{8,16},{16,24},{24,32},{32,40},{40,48},{48,56},{56,64},{64,7... | collective-permute-start | bytes 393224 | tf_op jit(solution)/shard_map/ppermute | solution.py:29
  124.8 6.9 %collective-permute-start.13 = (f32[32,1,1024]{2,0,1:T(8,128)S(1)}, f32[32,1,1024]{2,0,1:T(8,128)S(1)}, u32[]{:S(2)}, u32[]{:S(2)}) collective-permute-start(f32[32,1,1024]{2,0,1:T(8,128)S(1)} %get-tuple-element.60), channel_id=1, source_target_pairs={{8,0},{16,8},{24,16},{32,24},{40,32},{48,40},{56,48},{64,56},{72,6... | collective-permute-start | bytes 393224 | tf_op jit(solution)/shard_map/ppermute | solution.py:30
  138.0 200.5 %reduce-scatter.9.cloned.1.call-start = ((), (), s32[]{:S(2)}) async-start(), calls=%async_computation.6 | async-start | bytes 4718592 | tf_op jit(solution)/shard_map/reduce_scatter | solution.py:95
  195.5 6.9 %collective-permute-start.14 = (f32[1,4,1024]{2,0,1:T(1,128)S(1)}, f32[1,4,1024]{2,0,1:T(1,128)S(1)}, u32[]{:S(2)}, u32[]{:S(2)}) collective-permute-start(f32[1,4,1024]{2,0,1:T(1,128)S(1)} %get-tuple-element.57), channel_id=1, source_target_pairs={{0,1},{1,2},{2,3},{3,4},{4,5},{5,6},{6,7},{8,9},{9,10},{10,11},{11... | collective-permute-start | bytes 49160 | tf_op jit(solution)/shard_map/ppermute | solution.py:29
  205.2 6.0 collective-permute-start.16
  208.3 6.8 %collective-permute-start.17 = (f32[32,1,1024]{2,0,1:T(8,128)S(1)}, f32[32,1,1024]{2,0,1:T(8,128)S(1)}, u32[]{:S(2)}, u32[]{:S(2)}) collective-permute-start(f32[32,1,1024]{2,0,1:T(8,128)S(1)} %get-tuple-element.56), channel_id=1, source_target_pairs={{8,0},{16,8},{24,16},{32,24},{40,32},{48,40},{56,48},{64,56},{72,6... | collective-permute-start | bytes 393224 | tf_op jit(solution)/shard_map/ppermute | solution.py:30
  304.6 172.5 %reduce-scatter.11.cloned.1.call-start = ((), (), s32[]{:S(2)}) async-start(), calls=%async_computation.7 | async-start | bytes 4718592 | tf_op jit(solution)/shard_map/reduce_scatter | solution.py:103
  342.9 5.7 collective-permute-start.19
  354.0 5.7 collective-permute-start.21
  360.6 6.6 collective-permute-start.22
  365.2 5.7 collective-permute-start.23
  371.8 5.7 collective-permute-start.24
  375.5 5.7 collective-permute-start.25
  382.1 6.0 collective-permute-start.26
  386.2 5.7 collective-permute-start.27
  392.8 6.0 collective-permute-start.28
  396.8 5.7 collective-permute-start.29
  403.4 6.8 %collective-permute-start.30 = (f32[32,1,1024]{2,0,1:T(8,128)S(1)}, f32[32,1,1024]{2,0,1:T(8,128)S(1)}, u32[]{:S(2)}, u32[]{:S(2)}) collective-permute-start(f32[32,1,1024]{2,0,1:T(8,128)S(1)} %get-tuple-element.41), channel_id=1, source_target_pairs={{0,8},{8,16},{16,24},{24,32},{32,40},{40,48},{48,56},{56,64},{64,7... | collective-permute-start | bytes 393224 | tf_op jit(solution)/shard_map/ppermute | solution.py:29
  407.4 6.9 %collective-permute-start.31 = (f32[32,1,1024]{2,0,1:T(8,128)S(1)}, f32[32,1,1024]{2,0,1:T(8,128)S(1)}, u32[]{:S(2)}, u32[]{:S(2)}) collective-permute-start(f32[32,1,1024]{2,0,1:T(8,128)S(1)} %get-tuple-element.42), channel_id=1, source_target_pairs={{8,0},{16,8},{24,16},{32,24},{40,32},{48,40},{56,48},{64,56},{72,6... | collective-permute-start | bytes 393224 | tf_op jit(solution)/shard_map/ppermute | solution.py:30
  570.2 5.9 collective-permute-start.35
  (13 other events, 367.2 us)
Sparse Core Ops, SparseCore 0:
  14.7 41.2 reduce-scatter.4
  138.1 56.3 reduce-scatter.6
  304.7 33.7 reduce-scatter.8
  420.7 56.3 reduce-scatter.10
where the time goes:
time: 669 us; the launch traced here: 668 us
  waiting for transfers between devices  266 us (40%)
  blocking collectives  239 us (36%)
  starting transfers between devices  91.7 us (14%)
  other arithmetic  26.6 us (4%)
  matrix products  22.8 us (3%)
  between operations  18.6 us (3%)
    psum x2, blocking collectives, fit_sum(): return lax.psum(jnp.sum(current * precond), ('rows', 'days'))  159 us
    reduce_scatter x2, waiting for transfers between devices, from_modes(): lax.psum_scatter(jnp.einsum('kt,kxy->txy', local_basis, modes, precision=...  113 us
    psum x1, blocking collectives, body(): alpha = fit / lax.psum(jnp.sum(direction * image), ('rows', 'days'))  79.8 us
    reduce_scatter x2, waiting for transfers between devices, to_modes(): lax.psum_scatter(jnp.einsum('tk,txy->kxy', local_basis, field, precision=...  75.1 us
    ppermute x18, waiting for transfers between devices, with_halo(): after = lax.ppermute(leading, axis, down)  65.5 us
    ppermute x18, starting transfers between devices, with_halo(): before = lax.ppermute(last, axis, up)  64.5 us
    ppermute x18, starting transfers between devices, with_halo(): after = lax.ppermute(leading, axis, down)  27 us
  transfers between devices with their start and end apart: 40, of which 38 were waited for; matrix products, arithmetic and copies ran while one was open for 0% of the time, Pallas kernels for 0%

commit v1 on v0

v1 whole, which is shorter than its diff:
```python
import math

import jax
import jax.numpy as jnp
import numpy as np
from jax import lax
from jax.experimental import pallas as pl
from jax.experimental.pallas import tpu as pltpu
from jax.sharding import PartitionSpec as P

MESH = pl.DeviceIdType.MESH
DEG = 8
TIME_SHIFT = 0.05
HALF_OBS = 0.5
KAPPA_LOW = 0.02
KAPPA_HIGH = 2.0
WEIGHT_LOW = 0.5
WEIGHT_HIGH = 4.0
CENTRE_WEIGHT = 20.0 / 6.0
EDGE = 4.0 / 6.0
CORNER = 1.0 / 6.0
STENCIL_TOP = 16.0 / 3.0

Y = 4
TB = 32
RB = 4
COLS = 32
K = 4
LANES = 128


def modal_constants(total):
    order = np.arange(1, total + 1, dtype=np.float64)
    phase = np.outer(order, order) % (2 * (total + 1))
    basis = np.sqrt(2.0 / (total + 1)) * np.sin(np.pi * phase / (total + 1))
    basis = basis.astype(np.float32)
    high = basis.astype(jnp.bfloat16)
    low = (basis - high.astype(np.float32)).astype(jnp.bfloat16)
    eig = 2.0 + TIME_SHIFT - 2.0 * np.cos(np.pi * order / (total + 1))
    lower = eig * KAPPA_LOW + HALF_OBS * WEIGHT_LOW
    upper = eig * (KAPPA_HIGH + STENCIL_TOP) + HALF_OBS * WEIGHT_HIGH
    centre, spread = 0.5 * (upper + lower), 0.5 * (upper - lower)
    rows = np.zeros((8, total), np.float32)
    for at, row in enumerate((eig, 1.0 / centre, centre / spread, 1.0 / spread)):
        rows[at] = row
    return high, low, rows


def make_kernel(Z, D):
    NT = TB * D
    ROWS = RB * Y
    J = Y * D
    WIDE = NT // LANES

    def kernel(
        obs, mask, weight, classes, kappa, bh, bl, modal, sol, res,
        U, R, RES, G, ZH, QH, NAT, NATS, KC, HC, PR, PS, XR, XS,
        TZ, TQ, TW, TV, FZ, FQ, FW, FV, PW, CW, HW, HE, SW, SE, SA, RZ, SG, RG,
        halo_send, halo_recv, all_send, all_recv, cell_send, cell_recv, sum_send, sum_recv,
    ):
        ri, d = lax.axis_index("rows"), lax.axis_index("days")
        z, y = ri // Y, ri % Y
        j = y * D + jnp.where(y % 2 == 0, d, D - 1 - d)
        sub = lax.broadcasted_iota(jnp.int32, (8, NT), 0)

        def place(jt):
            yt, mt = jt // D, jt % D
            return yt, jnp.where(yt % 2 == 0, mt, D - 1 - mt)

        def device(zt, jt):
            yt, dt = place(jt)
            return (zt * Y + yt, dt)

        north, south = lax.rem(z + Z - 1, Z), lax.rem(z + 1, Z)
        west, east = lax.rem(j + J - 1, J), lax.rem(j + 1, J)

        def clear(i, c):
            U[i, 0] = jnp.zeros((K, 8, NT), jnp.float32)
            U[i, ROWS + 1] = jnp.zeros((K, 8, NT), jnp.float32)
            return c

        lax.fori_loop(0, 2, clear, 0)
        HW[...] = jnp.zeros_like(HW)
        HE[...] = jnp.zeros_like(HE)

        barrier = pltpu.get_barrier_semaphore()

        def greet(target):
            pl.semaphore_signal(barrier, inc=1, device_id=target, device_id_type=MESH)

        def greet_plane(i, c):
            greet(device(z, lax.rem(j + i, J)))
            return c

        def greet_column(i, c):
            greet((lax.rem(z + i, Z) * Y + y, d))
            return c

        lax.fori_loop(1, J, greet_plane, 0)
        lax.fori_loop(1, Z, greet_column, 0)
        for zt in (north, south):
            for jt in (west, east):
                greet(device(zt, jt))

        def swap(parts):
            lane = lax.broadcasted_iota(jnp.int32, parts[0].shape, 1)
            wide, even = lane < 64, (lane // 32) % 2 == 0
            t0 = jnp.where(wide, parts[0], pltpu.roll(parts[2], 64, 1))
            t2 = jnp.where(wide, pltpu.roll(parts[0], 64, 1), parts[2])
            t1 = jnp.where(wide, parts[1], pltpu.roll(parts[3], 64, 1))
            t3 = jnp.where(wide, pltpu.roll(parts[1], 64, 1), parts[3])
            d0 = jnp.where(even, t0, pltpu.roll(t1, 32, 1))
            d1 = jnp.where(even, pltpu.roll(t0, 96, 1), t1)
            d2 = jnp.where(even, t2, pltpu.roll(t3, 32, 1))
            d3 = jnp.where(even, pltpu.roll(t2, 96, 1), t3)
            return d0, d1, d2, d3

        slab = pl.ds(pl.multiple_of(d * LANES, LANES), LANES)
        cls = classes[:, slab]
        kap = jnp.zeros((RB, LANES), jnp.float32)
        for level in range(16):
            kap = jnp.where(cls == level, kappa[level], kap)
        own_w = weight[:, slab]
        sub8 = lax.broadcasted_iota(jnp.int32, (8, LANES), 0)
        cells = []
        for r in range(RB):
            w_row = jnp.broadcast_to(own_w[r : r + 1], (8, LANES))
            k_row = jnp.broadcast_to(kap[r : r + 1], (8, LANES))
            cells.append(jnp.where(sub8 == 0, w_row, k_row))
        for q, part in enumerate(swap(cells)):
            PW[q] = part

        pl.semaphore_wait(barrier, (J - 1) + (Z - 1) + 4)

        def cell_copy(q):
            return pltpu.make_async_remote_copy(
                src_ref=PW.at[q], dst_ref=CW.at[y], send_sem=cell_send.at[q],
                recv_sem=cell_recv.at[y], device_id=device(z, 4 * d + q), device_id_type=MESH,
            )

        def cell_local(q):
            return pltpu.make_async_copy(PW.at[q], CW.at[y], cell_recv.at[y])

        for q in range(4):
            @pl.when(4 * d + q != j)
            def _():
                cell_copy(q).start()

            @pl.when(4 * d + q == j)
            def _():
                cell_local(q).start()

        def to_tile(src, dst, at, i):
            jt = lax.rem(j + i, J)
            return pltpu.make_async_remote_copy(
                src_ref=src.at[jt], dst_ref=dst.at[y, pl.ds(pl.multiple_of(d * TB, TB), TB)],
                send_sem=all_send.at[at], recv_sem=all_recv.at[at],
                device_id=device(z, jt), device_id_type=MESH,
            )

        def to_days(src, dst, at, i):
            jt = lax.rem(j + i, J)
            yt, dt = place(jt)
            return pltpu.make_async_remote_copy(
                src_ref=src.at[yt, pl.ds(pl.multiple_of(dt * TB, TB), TB)], dst_ref=dst.at[j],
                send_sem=all_send.at[at], recv_sem=all_recv.at[at],
                device_id=device(z, jt), device_id_type=MESH,
            )

        def send_range(copy, src, dst, at, lo, hi):
            def one(i, c):
                copy(src, dst, at, i).start()
                return c

            lax.fori_loop(lo, hi, one, 0)

        def own_tile(src, dst, at):
            pltpu.make_async_copy(
                src.at[j], dst.at[y, pl.ds(pl.multiple_of(d * TB, TB), TB)], all_recv.at[at]
            ).start()

        def own_days(src, dst, at):
            pltpu.make_async_copy(
                src.at[y, pl.ds(pl.multiple_of(d * TB, TB), TB)], dst.at[j], all_recv.at[at]
            ).start()

        def all_wait(dst, at):
            pltpu.make_async_copy(dst, dst, all_recv.at[at]).wait()

        def all_wait_send(at):
            pltpu.make_async_copy(
                PR.at[pl.ds(0, J - 1)], PR.at[pl.ds(0, J - 1)], all_send.at[at]
            ).wait()

        def shuffle_seen(i, c):
            lanes = pl.ds(pl.multiple_of(i * LANES, LANES), LANES)
            seen, rhs = [], []
            for r in range(RB):
                s = mask[r, :, lanes].astype(jnp.float32) * weight[r : r + 1, lanes]
                seen.append(s)
                rhs.append(s * obs[r, :, lanes])
            for q, part in enumerate(swap(rhs)):
                PR[4 * i + q] = part
            for q, part in enumerate(swap(seen)):
                PS[4 * i + q] = part
            return c

        lax.fori_loop(0, J // 4, shuffle_seen, 0)
        own_tile(PR, XR, 0)
        send_range(to_tile, PR, XR, 0, 1, J)
        own_tile(PS, XS, 1)
        send_range(to_tile, PS, XS, 1, 1, J)

        for yt in range(Y):
            pltpu.make_async_copy(CW.at[yt], CW.at[yt], cell_recv.at[yt]).wait()

        def widen(v):
            return jnp.concatenate([v] * WIDE, axis=-1)

        def spread_cells(at, out, scale, shift):
            for yt in range(Y):
                flat = jnp.broadcast_to(CW[yt][at : at + 1], (LANES, LANES)) * scale + shift
                turned = jnp.transpose(flat).reshape(RB, COLS, LANES)
                NAT[0, yt * RB : (yt + 1) * RB] = turned

            def one(r, c):
                for k in range(K):
                    out[r, k] = NAT[0, r, pl.ds(k, 8, stride=K), :]
                return c

            lax.fori_loop(0, ROWS, one, 0)

        spread_cells(0, HC, HALF_OBS, 0.0)
        spread_cells(1, KC, 1.0, CENTRE_WEIGHT)

        def load_natural(ref, r, k):
            return jnp.concatenate([ref[w, r, pl.ds(k, 8, stride=K), :] for w in range(WIDE)], axis=-1)

        def store_natural(ref, r, k, v):
            for w in range(WIDE):
                ref[w, r, pl.ds(k, 8, stride=K), :] = v[:, w * LANES : (w + 1) * LANES]

        def split(v):
            high = v.astype(jnp.bfloat16)
            return high, (v - high.astype(jnp.float32)).astype(jnp.bfloat16)

        def dot(a, b, dims):
            return lax.dot_general(a, b, (dims, ((), ())), preferred_element_type=jnp.float32)

        def to_modes(tile):
            def one(i, c):
                v = jnp.concatenate([tile(2 * i), tile(2 * i + 1)], axis=1)
                high, low = split(jnp.transpose(v))
                dims = ((1,), (0,))
                h = dot(high, bh[...], dims) + (dot(high, bl[...], dims) + dot(low, bh[...], dims))
                for w in range(WIDE):
                    half = h[:, w * LANES : (w + 1) * LANES]
                    NAT[w, pl.ds(2 * RB * i, 2 * RB)] = half.reshape(2 * RB, COLS, LANES)
                return c

            lax.fori_loop(0, Y // 2, one, 0)

        def to_time(out):
            def one(i, c):
                v = [NATS[w, pl.ds(2 * RB * i, 2 * RB)].reshape(2 * RB * COLS, LANES) for w in range(WIDE)]
                v = jnp.concatenate(v, axis=1)
                high, low = split(v)
                dims = ((1,), (1,))
                t = dot(bh[...], high, dims) + (dot(bl[...], high, dims) + dot(bh[...], low, dims))
                out[2 * i] = t[:, :LANES]
                out[2 * i + 1] = t[:, LANES:]
                return c

            lax.fori_loop(0, Y // 2, one, 0)

        def halo(p):
            def copy(at, src, dst, target):
                return pltpu.make_async_remote_copy(
                    src_ref=src, dst_ref=dst, send_sem=halo_send.at[p, at],
                    recv_sem=halo_recv.at[p, at], device_id=target, device_id_type=MESH,
                )

            top, bottom, left, right = z == 0, z == Z - 1, j == 0, j == J - 1
            dump = ROWS + 2
            far = dump + ROWS
            first = [
                copy(0, U.at[p, 1], U.at[p, jnp.where(top, dump, ROWS + 1)], device(north, j)),
                copy(1, U.at[p, ROWS], U.at[p, jnp.where(bottom, dump, 0)], device(south, j)),
                copy(2, SW.at[p, 0], HE.at[p, jnp.where(top | left, far, ROWS + 1)], device(north, west)),
                copy(3, SE.at[p, 0], HW.at[p, jnp.where(top | right, far, ROWS + 1)], device(north, east)),
                copy(4, SW.at[p, ROWS - 1], HE.at[p, jnp.where(bottom | left, far + 1, 0)], device(south, west)),
                copy(5, SE.at[p, ROWS - 1], HW.at[p, jnp.where(bottom | right, far + 1, 0)], device(south, east)),
            ]
            second = [
                copy(6, SW.at[p], HE.at[p, pl.ds(jnp.where(left, dump, 1), ROWS)], device(z, west)),
                copy(7, SE.at[p], HW.at[p, pl.ds(jnp.where(right, dump, 1), ROWS)], device(z, east)),
            ]
            return first, second

        def halo_wait(p):
            first, second = halo(p)
            for copy in first + second:
                copy.wait()

        def run_rows(q, row, carry):
            first, second = halo(q)
            carry = lax.fori_loop(0, 2, lambda i, c: row(i * (ROWS - 1), c), carry)
            for copy in first:
                copy.start()
            carry = lax.fori_loop(1, ROWS - 1, row, carry)
            for copy in second:
                copy.start()
            return carry

        def put_update(q, r, k, v):
            U[q, r + 1, k] = v
            if k == 0:
                SW[q, r] = v[0:1]
            if k == K - 1:
                SE[q, r] = v[7:8]

        eig = modal[0:1]
        inv_centre = modal[1:2]
        stretch = modal[2:3]
        inv_spread = modal[3:4]

        def apply_row(p, r):
            v = [U[p, r + 1, k] for k in range(K)]
            s = [U[p, r, k] + U[p, r + 2, k] for k in range(K)]
            a = [EDGE * v[k] + CORNER * s[k] for k in range(K)]
            wl = EDGE * HW[p, r + 1] + CORNER * (HW[p, r] + HW[p, r + 2])
            er = EDGE * HE[p, r + 1] + CORNER * (HE[p, r] + HE[p, r + 2])
            before = jnp.where(sub == 0, wl, pltpu.roll(a[K - 1], 1, 0))
            after = jnp.where(sub == 7, er, pltpu.roll(a[0], 7, 0))
            row = [before] + a + [after]
            out = []
            for k in range(K):
                h = row[k] + row[k + 2] + EDGE * s[k]
                hc = widen(HC[r, k])
                out.append((eig * (widen(KC[r, k]) * v[k] - h) + hc * v[k], v[k], hc))
            return out

        def start_row(src):
            def row(r, c):
                for k in range(K):
                    g = load_natural(src, r, k)
                    G[r, k] = g
                    R[r, k] = g
                    u = g * inv_centre
                    RES[r, k] = u
                    put_update(0, r, k, u)
                return c

            return row

        def sweep(p, ratio):
            ratio_next = 1.0 / (2.0 * stretch - ratio)
            ca, cb = ratio_next * ratio, 2.0 * ratio_next * inv_spread

            def row(r, c):
                for k, (dv, v, _) in enumerate(apply_row(p, r)):
                    rem = R[r, k] - dv
                    R[r, k] = rem
                    u = ca * v + cb * rem
                    RES[r, k] = RES[r, k] + u
                    put_update(1 - p, r, k, u)
                return c

            halo_wait(p)
            run_rows(1 - p, row, 0)
            return ratio_next

        def sweeps(lo, hi, ratio, extra=None):
            def one(n, ratio):
                ratio = sweep(n % 2, ratio)
                if extra is not None:
                    extra(n)
                return ratio

            return lax.fori_loop(lo, hi, one, ratio)

        def natural(src):
            def one(r, c):
                for k in range(K):
                    store_natural(NATS, r, k, src[r, k])
                return c

            lax.fori_loop(0, ROWS, one, 0)

        def fold(v):
            v = jnp.sum(v, axis=0, keepdims=True)
            out = v[:, :LANES]
            for i in range(1, WIDE):
                out = out + v[:, i * LANES : (i + 1) * LANES]
            return jnp.broadcast_to(out, (8, LANES))

        def pack(parts):
            out = fold(parts[0])
            for at, part in enumerate(parts[1:], 1):
                out = jnp.where(sub8 == at, fold(part), out)
            return out

        def column_copy(at, i):
            return pltpu.make_async_remote_copy(
                src_ref=SA.at[at], dst_ref=RZ.at[at, z], send_sem=sum_send.at[at, 0],
                recv_sem=sum_recv.at[at, 0],
                device_id=(lax.rem(z + i, Z) * Y + y, d), device_id_type=MESH,
            )

        def plane_copy(at, i):
            return pltpu.make_async_remote_copy(
                src_ref=SG.at[at], dst_ref=RG.at[at, j], send_sem=sum_send.at[at, 1],
                recv_sem=sum_recv.at[at, 1],
                device_id=device(z, lax.rem(j + i, J)), device_id_type=MESH,
            )

        def wait_bytes(ref, count, sem):
            part = ref.at[pl.ds(0, count)]
            pltpu.make_async_copy(part, part, sem).wait()

        def column_start(at, value):
            SA[at] = value
            RZ[at, z] = value

            def one(i, c):
                column_copy(at, i).start()
                return c

            lax.fori_loop(1, Z, one, 0)

        def column_end(at):
            for side in (sum_recv, sum_send):
                wait_bytes(RZ.at[at], Z - 1, side.at[at, 0])
            return lax.fori_loop(1, Z, lambda i, c: c + RZ[at, i], RZ[at, 0])

        def plane_start(at, value):
            SG[at] = value
            RG[at, j] = value

            def one(i, c):
                plane_copy(at, i).start()
                return c

            lax.fori_loop(1, J, one, 0)

        def plane_end(at):
            for side in (sum_recv, sum_send):
                wait_bytes(RG.at[at], J - 1, side.at[at, 1])
            total = lax.fori_loop(1, J, lambda i, c: c + RG[at, i], RG[at, 0])
            return [jnp.sum(total[i : i + 1], axis=1, keepdims=True) for i in range(3)]

        zero = jnp.zeros((8, NT), jnp.float32)

        all_wait(XR, 0)
        to_modes(lambda i: XR[i])
        run_rows(0, start_row(NAT), 0)
        ratio = sweeps(0, DEG - 1, 1.0 / stretch)
        natural(RES)
        to_time(TZ)
        all_wait(XS, 1)
        to_modes(lambda i: TZ[i] * XS[i])
        p = (DEG - 1) % 2

        def first_image(r, acc):
            fit, curve = acc
            for k, (dv, v, hc) in enumerate(apply_row(p, r)):
                g, zh = G[r, k], RES[r, k]
                q = g - (R[r, k] - dv) - hc * zh + load_natural(NAT, r, k)
                ZH[r, k] = zh
                QH[r, k] = q
                store_natural(NATS, r, k, q)
                R[r, k] = q
                u = q * inv_centre
                RES[r, k] = u
                put_update(1 - p, r, k, u)
                fit, curve = fit + g * zh, curve + zh * q
            return fit, curve

        halo_wait(p)
        fit, curve = run_rows(1 - p, first_image, (zero, zero))
        column_start(0, pack([fit, curve]))
        to_time(TQ)
        own_days(TZ, FZ, 2)
        own_days(TQ, FQ, 3)

        def trickle(n):
            lo, hi = 1 + n * (J - 1) // (DEG - 1), 1 + (n + 1) * (J - 1) // (DEG - 1)
            send_range(to_days, TZ, FZ, 2, lo, hi)
            send_range(to_days, TQ, FQ, 3, lo, hi)

        ratio = sweeps(0, 2, 1.0 / stretch, trickle)
        plane_start(0, column_end(0))
        ratio = sweeps(2, DEG - 1, ratio, trickle)
        natural(RES)
        to_time(TW)
        own_days(TW, FW, 4)
        send_range(to_days, TW, FW, 4, 1, J)
        to_modes(lambda i: TW[i] * XS[i])
        fit0, curve0, _ = plane_end(0)
        alpha0 = fit0 / curve0

        def second_image(r, acc):
            fit, curve, cross = acc
            for k, (dv, v, hc) in enumerate(apply_row(p, r)):
                g, wh, zh = QH[r, k], RES[r, k], ZH[r, k]
                q = g - (R[r, k] - dv) - hc * wh + load_natural(NAT, r, k)
                store_natural(NATS, r, k, q)
                z1 = zh - alpha0 * wh
                fit = fit + (G[r, k] - alpha0 * g) * z1
                curve = curve + z1 * (g - alpha0 * q)
                cross = cross + z1 * g
            return fit, curve, cross

        halo_wait(p)
        sums = lax.fori_loop(0, ROWS, second_image, (zero, zero, zero))
        column_start(1, pack(sums))
        to_time(TV)
        own_days(TV, FV, 5)
        send_range(to_days, TV, FV, 5, 1, J)
        plane_start(1, column_end(1))
        fit1, curve1, cross1 = plane_end(1)
        beta = fit1 / fit0
        alpha1 = fit1 / (curve1 + 2.0 * beta * cross1 + beta * beta * curve0)
        c_old = alpha0 + alpha1 + alpha1 * beta
        c_new = alpha0 * alpha1

        for at, dst in ((2, FZ), (3, FQ), (4, FW)):
            all_wait(dst, at)

        def finish(i, c):
            lanes = pl.ds(pl.multiple_of(i * LANES, LANES), LANES)
            for part, out in enumerate((sol, res)):
                values = []
                for q in range(4):
                    at = 4 * i + q
                    if part == 0:
                        values.append(c_old * FZ[at] - c_new * FW[at])
                    else:
                        values.append(PR[at] - c_old * FQ[at] + c_new * FV[at])
                for r, v in enumerate(swap(values)):
                    out[r, :, lanes] = v
            return c

        all_wait(FV, 5)
        lax.fori_loop(0, J // 4, finish, 0)

        for at in range(6):
            all_wait_send(at)
        for q in range(4):
            @pl.when(4 * d + q != j)
            def _():
                cell_copy(q).wait_send()

    f32 = jnp.float32
    field = pltpu.VMEM((ROWS, K, 8, NT), f32)
    flat = pltpu.VMEM((WIDE, ROWS, COLS, LANES), f32)
    cell = pltpu.VMEM((ROWS, K, 8, LANES), f32)
    days = pltpu.VMEM((J, TB, LANES), f32)
    tile = pltpu.VMEM((Y, NT, LANES), f32)
    edge = pltpu.VMEM((2, 2 * ROWS + 4, 1, NT), f32)
    side = pltpu.VMEM((2, ROWS, 1, NT), f32)
    scratch = [
        pltpu.VMEM((2, ROWS + 3, K, 8, NT), f32), field, field, field, field, field, flat, flat,
        cell, cell, days, days, tile, tile, tile, tile, tile, tile, days, days, days, days,
        pltpu.VMEM((4, 8, LANES), f32), pltpu.VMEM((Y, 8, LANES), f32), edge, edge, side, side,
        pltpu.VMEM((2, 8, LANES), f32), pltpu.VMEM((2, Z, 8, LANES), f32),
        pltpu.VMEM((2, 8, LANES), f32), pltpu.VMEM((2, J, 8, LANES), f32),
        pltpu.SemaphoreType.DMA((2, 8)), pltpu.SemaphoreType.DMA((2, 8)),
        pltpu.SemaphoreType.DMA((6,)), pltpu.SemaphoreType.DMA((6,)),
        pltpu.SemaphoreType.DMA((4,)), pltpu.SemaphoreType.DMA((Y,)),
        pltpu.SemaphoreType.DMA((2, 2)), pltpu.SemaphoreType.DMA((2, 2)),
    ]
    return kernel, scratch


def solution(mesh):
    Z = mesh.shape["rows"] // Y
    D = mesh.shape["days"]
    kernel, scratch = make_kernel(Z, D)
    high, low, modal = modal_constants(TB * D)
    vmem = pl.BlockSpec(memory_space=pltpu.VMEM)
    smem = pl.BlockSpec(memory_space=pltpu.SMEM)

    def body(observations, obs_mask, obs_weight, classes, kappa_table):
        shape = jax.ShapeDtypeStruct((RB, TB, COLS * Y * D), jnp.float32)
        sol, res = pl.pallas_call(
            kernel,
            out_shape=(shape, shape),
            in_specs=[vmem] * 4 + [smem] + [vmem] * 3,
            out_specs=(vmem, vmem),
            scratch_shapes=scratch,
            compiler_params=pltpu.CompilerParams(
                collective_id=0, has_side_effects=True, vmem_limit_bytes=48 * 1024 * 1024
            ),
        )(
            jnp.transpose(observations, (1, 0, 2)), jnp.transpose(obs_mask, (1, 0, 2)),
            obs_weight, classes, kappa_table, jnp.asarray(high), jnp.asarray(low), jnp.asarray(modal),
        )
        return jnp.transpose(sol, (1, 0, 2)), jnp.transpose(res, (1, 0, 2))

    in_specs = (P("days", "rows", None), P("days", "rows", None), P("rows", None), P("rows", None), P())
    out_specs = (P("days", "rows", None), P("days", "rows", None))
    return jax.shard_map(body, mesh=mesh, in_specs=in_specs, out_specs=out_specs, check_vma=False)
```

time: 669 us -> 124 us (0.19)
  waiting for transfers between devices: 266 us -> 0 us
  blocking collectives: 239 us -> 0 us
  Pallas kernels: 0 us -> 118 us
  starting transfers between devices: 91.7 us -> 0 us
  other arithmetic: 26.6 us -> 0 us
  matrix products: 22.8 us -> 0 us
  between operations: 18.6 us -> 0.71 us
    psum x3 -> x0, blocking collectives: 239 us -> none  [the longest x2 159 us: fit_sum(): return lax.psum(jnp.sum(current * precond), ('rows', 'days'))]
    reduce_scatter x4 -> x0, waiting for transfers between devices: 188 us -> none  [the longest x2 113 us: from_modes(): lax.psum_scatter(jnp.einsum('kt,kxy->txy', local_basis, modes, precision=...]
    pallas_call x0 -> x1, Pallas kernels: none -> 118 us  [body(): pl.pallas_call(kernel, out_shape=(shape, shape), in_specs=[vmem] * 4 + [s...]
    ppermute x36 -> x0, starting transfers between devices: 91.5 us -> none  [the longest x18 64.5 us: with_halo(): before = lax.ppermute(last, axis, up)]
    ppermute x36 -> x0, waiting for transfers between devices: 77.4 us -> none  [the longest x18 65.5 us: with_halo(): after = lax.ppermute(leading, axis, down)]
    dot_general x4 -> x0, matrix products: 22.8 us -> none  [the longest x2 11.8 us: from_modes(): jnp.einsum('kt,kxy->txy', local_basis, modes, precision=lax.Precision.HIG...]
    add x16 -> x0, other arithmetic: 9.83 us -> none  [the longest x12 8.65 us: chebyshev(): update = ratio_next * ratio * update + 2.0 * ratio_next / spread * remainder]
  transfers between devices with their start and end apart: 40 -> 0, of which waited for: 38 -> 0; matrix products, arithmetic and copies ran while one was open for 0% -> 0% of each run, Pallas kernels for 0% -> 0%
where the time goes in v1:
time: 124 us
  Pallas kernels  118 us (95%)
  local copies, waits for them, and re-layouts  4.69 us (4%)
    pallas_call x1, Pallas kernels, body(): pl.pallas_call(kernel, out_shape=(shape, shape), in_specs=[vmem] * 4 + [s...  118 us
    unnamed x18, local copies, waits for them, and re-layouts  4.69 us

profile of v1, /device:TPU:1, one launch (start us, length us, event | category | flops | bytes accessed | tf_op | source)
XLA Modules:
  0.0 123.5 jit_solution(12685579931342546865)
XLA Ops:
  0.6 0.0 copy-start.6
  0.6 1.4 %copy.17 = f32[32,4,1024]{2,0,1:T(8,128)S(1)} copy(f32[32,4,1024]{2,1,0:T(4,128)} %param.8) | data formatting | bytes 1048576 | tf_op args[0]
  2.0 0.0 copy-done.6
  2.1 0.0 copy-start
  2.1 0.0 copy-start.1
  2.1 0.0 copy-start.2
  2.1 0.0 copy-start.3
  2.1 0.0 copy-start.4
  2.1 0.3 copy.16
  2.4 0.0 copy-start.5
  2.4 0.5 copy-done
  3.0 0.1 copy-done.1
  3.0 0.0 copy-done.2
  3.0 0.0 copy-done.3
  3.0 0.0 copy-done.4
  3.0 0.1 copy-done.5
  3.1 118.1 %shard_map.95 = (f32[4,32,1024]{2,1,0:T(8,128)S(1)}, f32[4,32,1024]{2,1,0:T(8,128)S(1)}) custom-call(f32[4,32,1024]{2,1,0:T(8,128)S(1)} %bitcast.8, s32[4,32,1024]{2,1,0:T(8,128)S(1)} %bitcast.9, f32[4,1024]{1,0:T(4,128)S(1)} %copy-done.2, s32[4,1024]{1,0:T(4,128)S(1)} %copy-done.3, f32[16]{0:T(128)S(1)} %copy-done.5, bf16[256,256]{1,0:T(8,128)(2,1)S(1)} %copy-done.1, ...), custom_call_target="tpu_custom_call" | custom-call | tf_op jit(solution)/shard_map/pallas_call | solution.py:586
  121.3 1.1 copy.12
  122.4 1.1 copy.13
Async XLA Ops:
  0.6 1.4 %copy-start.6 = (s32[32,4,1024]{2,1,0:T(4,128)S(1)}, s32[32,4,1024]{2,1,0:T(4,128)}, u32[]{:S(2)}) copy-start(s32[32,4,1024]{2,1,0:T(4,128)} %param.9) | copy-start | bytes 1572868
  2.1 0.9 copy-start
  2.1 1.0 copy-start.1
  2.1 1.0 copy-start.2
  2.1 0.9 copy-start.3
  2.1 0.9 copy-start.4
  2.4 0.7 copy-start.5

commit v2 on v1

v2 whole, which is shorter than its diff:
```python
import math

import jax
import jax.numpy as jnp
import numpy as np
from jax import lax
from jax.experimental import pallas as pl
from jax.experimental.pallas import tpu as pltpu
from jax.sharding import PartitionSpec as P

MESH = pl.DeviceIdType.MESH
DEG = 8
TIME_SHIFT = 0.05
HALF_OBS = 0.5
KAPPA_LOW = 0.02
KAPPA_HIGH = 2.0
WEIGHT_LOW = 0.5
WEIGHT_HIGH = 4.0
STENCIL_SCALE = 6.0
STENCIL_TOP = 16.0 / 3.0

Y = 4
TB = 32
RB = 4
COLS = 32
HALO = 8
K = (COLS + 2 * HALO) // 8
LANES = 128


def modal_constants(total):
    order = np.arange(1, total + 1, dtype=np.float64)
    phase = np.outer(order, order) % (2 * (total + 1))
    basis = np.sqrt(2.0 / (total + 1)) * np.sin(np.pi * phase / (total + 1))
    eig = 2.0 + TIME_SHIFT - 2.0 * np.cos(np.pi * order / (total + 1))
    lower = eig * KAPPA_LOW + HALF_OBS * WEIGHT_LOW
    upper = eig * (KAPPA_HIGH + STENCIL_TOP) + HALF_OBS * WEIGHT_HIGH
    centre, spread = 0.5 * (upper + lower), 0.5 * (upper - lower)
    rows = np.zeros((8, total), np.float32)
    for at, row in enumerate((eig / STENCIL_SCALE, 1.0 / centre, centre / spread, 1.0 / spread)):
        rows[at] = row
    return basis.astype(np.float32), rows


def make_kernel(Z, D):
    NT = TB * D
    ROWS = RB * Y
    J = Y * D
    WIDE = NT // LANES
    ER, EC = ROWS + 2 * HALO, COLS + 2 * HALO
    OWN = pl.ds(HALO, COLS)

    def kernel(
        obs, mask, weight, classes, kappa, basis, modal, sol, res,
        GE1, GE2, U, G, KC, HC, NC, MK, NAT, NQ, NZ, NW, NV, PR, PS, XR, XS,
        TZ, TQ, TW, TV, FZ, FQ, FW, FV, PW, CW, CT, CN, SA, RZ, SG, RG,
        halo_send, halo_recv, near_send, near_recv, all_send, all_recv, cell_send, cell_recv,
        sum_send, sum_recv,
    ):
        ri, d = lax.axis_index("rows"), lax.axis_index("days")
        z, y = ri // Y, ri % Y
        j = y * D + jnp.where(y % 2 == 0, d, D - 1 - d)
        top, bottom, left, right = z == 0, z == Z - 1, j == 0, j == J - 1

        def place(jt):
            yt, mt = jt // D, jt % D
            return yt, jnp.where(yt % 2 == 0, mt, D - 1 - mt)

        def device(zt, jt):
            yt, dt = place(jt)
            return (zt * Y + yt, dt)

        north, south = lax.rem(z + Z - 1, Z), lax.rem(z + 1, Z)
        west, east = lax.rem(j + J - 1, J), lax.rem(j + 1, J)

        CN[...] = jnp.zeros_like(CN)
        for cond, rows, cols in (
            (top, pl.ds(0, HALO), pl.ds(0, EC)),
            (bottom, pl.ds(HALO + ROWS, HALO), pl.ds(0, EC)),
            (left, pl.ds(0, ER), pl.ds(0, HALO)),
            (right, pl.ds(0, ER), pl.ds(HALO + COLS, HALO)),
        ):
            @pl.when(cond)
            def _():
                for ge in (GE1, GE2):
                    for w in range(WIDE):
                        ge[w, rows, cols, :] = jnp.zeros((rows.size, cols.size, LANES), jnp.float32)

        barrier = pltpu.get_barrier_semaphore()

        def greet(target):
            pl.semaphore_signal(barrier, inc=1, device_id=target, device_id_type=MESH)

        def greet_plane(i, c):
            greet(device(z, lax.rem(j + i, J)))
            return c

        def greet_column(i, c):
            greet((lax.rem(z + i, Z) * Y + y, d))
            return c

        lax.fori_loop(1, J, greet_plane, 0)
        lax.fori_loop(1, Z, greet_column, 0)
        for zt in (north, south):
            for jt in (west, east):
                greet(device(zt, jt))

        def swap(parts):
            lane = lax.broadcasted_iota(jnp.int32, parts[0].shape, 1)
            wide, even = lane < 64, (lane // 32) % 2 == 0
            t0 = jnp.where(wide, parts[0], pltpu.roll(parts[2], 64, 1))
            t2 = jnp.where(wide, pltpu.roll(parts[0], 64, 1), parts[2])
            t1 = jnp.where(wide, parts[1], pltpu.roll(parts[3], 64, 1))
            t3 = jnp.where(wide, pltpu.roll(parts[1], 64, 1), parts[3])
            d0 = jnp.where(even, t0, pltpu.roll(t1, 32, 1))
            d1 = jnp.where(even, pltpu.roll(t0, 96, 1), t1)
            d2 = jnp.where(even, t2, pltpu.roll(t3, 32, 1))
            d3 = jnp.where(even, pltpu.roll(t2, 96, 1), t3)
            return d0, d1, d2, d3

        slab = pl.ds(pl.multiple_of(d * LANES, LANES), LANES)
        cls = classes[:, slab]
        kap = jnp.zeros((RB, LANES), jnp.float32)
        for level in range(16):
            kap = jnp.where(cls == level, kappa[level], kap)
        own_w = weight[:, slab]
        sub8 = lax.broadcasted_iota(jnp.int32, (8, LANES), 0)
        cells = []
        for r in range(RB):
            w_row = jnp.broadcast_to(own_w[r : r + 1], (8, LANES))
            k_row = jnp.broadcast_to(kap[r : r + 1], (8, LANES))
            cells.append(jnp.where(sub8 == 0, w_row, k_row))
        for q, part in enumerate(swap(cells)):
            PW[q] = part

        def shuffle_seen(i, c):
            lanes = pl.ds(pl.multiple_of(i * LANES, LANES), LANES)
            seen, rhs = [], []
            for r in range(RB):
                s = mask[r, :, lanes].astype(jnp.float32) * weight[r : r + 1, lanes]
                seen.append(s)
                rhs.append(s * obs[r, :, lanes])
            for q, part in enumerate(swap(rhs)):
                PR[4 * i + q] = part
            for q, part in enumerate(swap(seen)):
                PS[4 * i + q] = part
            return c

        lax.fori_loop(0, J // 4, shuffle_seen, 0)
        U[...] = jnp.zeros_like(U)

        pl.semaphore_wait(barrier, (J - 1) + (Z - 1) + 4)

        def cell_copy(q):
            return pltpu.make_async_remote_copy(
                src_ref=PW.at[q], dst_ref=CW.at[y], send_sem=cell_send.at[q],
                recv_sem=cell_recv.at[y], device_id=device(z, 4 * d + q), device_id_type=MESH,
            )

        def cell_local(q):
            return pltpu.make_async_copy(PW.at[q], CW.at[y], cell_recv.at[y])

        for q in range(4):
            @pl.when(4 * d + q != j)
            def _():
                cell_copy(q).start()

            @pl.when(4 * d + q == j)
            def _():
                cell_local(q).start()

        def to_tile(src, dst, at, i):
            jt = lax.rem(j + i, J)
            return pltpu.make_async_remote_copy(
                src_ref=src.at[jt], dst_ref=dst.at[y, pl.ds(pl.multiple_of(d * TB, TB), TB)],
                send_sem=all_send.at[at], recv_sem=all_recv.at[at],
                device_id=device(z, jt), device_id_type=MESH,
            )

        def to_days(src, dst, at, i):
            jt = lax.rem(j + i, J)
            yt, dt = place(jt)
            return pltpu.make_async_remote_copy(
                src_ref=src.at[yt, pl.ds(pl.multiple_of(dt * TB, TB), TB)], dst_ref=dst.at[j],
                send_sem=all_send.at[at], recv_sem=all_recv.at[at],
                device_id=device(z, jt), device_id_type=MESH,
            )

        def send_all(copy, src, dst, at):
            def one(i, c):
                copy(src, dst, at, i).start()
                return c

            lax.fori_loop(1, J, one, 0)

        def send_tile(src, dst, at):
            send_all(to_tile, src, dst, at)
            pltpu.make_async_copy(
                src.at[j], dst.at[y, pl.ds(pl.multiple_of(d * TB, TB), TB)], all_recv.at[at]
            ).start()

        def send_days(src, dst, at):
            send_all(to_days, src, dst, at)
            pltpu.make_async_copy(
                src.at[y, pl.ds(pl.multiple_of(d * TB, TB), TB)], dst.at[j], all_recv.at[at]
            ).start()

        def all_wait(dst, at):
            pltpu.make_async_copy(dst, dst, all_recv.at[at]).wait()

        def all_wait_send(at):
            pltpu.make_async_copy(
                PR.at[pl.ds(0, J - 1)], PR.at[pl.ds(0, J - 1)], all_send.at[at]
            ).wait()

        ways = []
        for dz, dj in ((-1, 0), (1, 0), (0, -1), (0, 1), (-1, -1), (-1, 1), (1, -1), (1, 1)):
            to_ok, from_ok = True, True
            if dz:
                to_ok, from_ok = (~top, ~bottom) if dz < 0 else (~bottom, ~top)
            if dj:
                a, b = (~left, ~right) if dj < 0 else (~right, ~left)
                to_ok, from_ok = (a, b) if to_ok is True else (to_ok & a, from_ok & b)
            zt = z if dz == 0 else (north if dz < 0 else south)
            jt = j if dj == 0 else (west if dj < 0 else east)
            ways.append((dz, dj, device(zt, jt), to_ok, from_ok))

        def near_copy(at):
            return pltpu.make_async_remote_copy(
                src_ref=CT, dst_ref=CN.at[at], send_sem=near_send.at[at],
                recv_sem=near_recv.at[at], device_id=ways[at][2], device_id_type=MESH,
            )

        def halo_copy(ge, n, w, at):
            dz, dj, target, _, _ = ways[at]
            def span(delta, size):
                if delta == 0:
                    return pl.ds(HALO, size), pl.ds(HALO, size)
                if delta < 0:
                    return pl.ds(HALO, HALO), pl.ds(HALO + size, HALO)
                return pl.ds(size, HALO), pl.ds(0, HALO)

            (rs, rd), (cs, cd) = span(dz, ROWS), span(dj, COLS)
            return pltpu.make_async_remote_copy(
                src_ref=ge.at[w, rs, cs], dst_ref=ge.at[w, rd, cd],
                send_sem=halo_send.at[n, w, at], recv_sem=halo_recv.at[n, w, at],
                device_id=target, device_id_type=MESH,
            )

        def each_way(which, do):
            for at, way in enumerate(ways):
                @pl.when(way[which])
                def _():
                    do(at)

        def halo_start(ge, n, w):
            each_way(3, lambda at: halo_copy(ge, n, w, at).start())

        def halo_wait(ge, n, w):
            each_way(4, lambda at: halo_copy(ge, n, w, at).wait_recv())

        send_tile(PR, XR, 0)

        for yt in range(Y):
            pltpu.make_async_copy(CW.at[yt], CW.at[yt], cell_recv.at[yt]).wait()
        packed = jnp.zeros((8, LANES), jnp.float32)
        for yt in range(Y):
            for f in range(2):
                packed = jnp.where(sub8 == Y * f + yt, CW[yt][f : f + 1], packed)
        CT[...] = packed
        each_way(3, lambda at: near_copy(at).start())

        column = lax.broadcasted_iota(jnp.int32, (8, LANES), 0) * K
        for k in range(K):
            outside = (left & (column + k < HALO)) | (right & (column + k >= HALO + COLS))
            MK[k] = jnp.where(outside, 0.0, 1.0)

        def spread_tile(source, dz, dj):
            for f, scale, shift in ((0, HALF_OBS, 0.0), (1, STENCIL_SCALE, 20.0)):
                for yt in range(Y):
                    if (dz < 0 and RB * (yt + 1) <= ROWS - HALO) or (dz > 0 and RB * yt >= HALO):
                        continue
                    at = Y * f + yt
                    flat = jnp.broadcast_to(source[at : at + 1], (LANES, LANES)) * scale + shift
                    turned = jnp.transpose(flat).reshape(RB, COLS, LANES)
                    row = HALO + dz * ROWS + RB * yt
                    if dj == 0:
                        NC[f, row : row + RB, OWN, :] = turned
                    elif dj < 0:
                        NC[f, row : row + RB, 0:HALO, :] = turned[:, COLS - HALO :]
                    else:
                        NC[f, row : row + RB, HALO + COLS : EC, :] = turned[:, :HALO]

        spread_tile(packed, 0, 0)
        each_way(4, lambda at: near_copy(at).wait_recv())
        for at, way in enumerate(ways):
            spread_tile(CN[at], -way[0], -way[1])

        def interleave_cells(e, c):
            for k in range(K):
                HC[e, k] = NC[0, e, pl.ds(k, 8, stride=K), :]
                KC[e, k] = NC[1, e, pl.ds(k, 8, stride=K), :]
            return c

        lax.fori_loop(0, ER, interleave_cells, 0)

        def dot(a, b, dims):
            return lax.dot_general(
                a, b, (dims, ((), ())), precision=lax.Precision.HIGHEST,
                preferred_element_type=jnp.float32,
            )

        def to_modes(tile, put):
            def one(i, c):
                v = jnp.concatenate([tile(2 * i), tile(2 * i + 1)], axis=1)
                h = dot(jnp.transpose(v), basis[...], ((1,), (0,)))
                for w in range(WIDE):
                    put(w, 2 * RB * i, h[:, w * LANES : (w + 1) * LANES].reshape(2 * RB, COLS, LANES))
                return c

            lax.fori_loop(0, Y // 2, one, 0)

        def to_time(get, out):
            def one(i, c):
                v = [get(w, pl.ds(2 * RB * i, 2 * RB)).reshape(2 * RB * COLS, LANES) for w in range(WIDE)]
                t = dot(basis[...], jnp.concatenate(v, axis=1), ((1,), (1,)))
                out[2 * i] = t[:, :LANES]
                out[2 * i + 1] = t[:, LANES:]
                return c

            lax.fori_loop(0, Y // 2, one, 0)

        def full(v):
            return jnp.broadcast_to(v, (8, LANES))

        def coefficients(w):
            lanes = slice(w * LANES, (w + 1) * LANES)
            return [modal[i : i + 1, lanes] for i in range(4)]

        def stencil(p, w, u):
            v = [U[p, w, u, k] for k in range(K)]
            s = [U[p, w, u - 1, k] + U[p, w, u + 1, k] for k in range(K)]
            a = [4.0 * v[k] + s[k] for k in range(K)]
            row = [pltpu.roll(a[K - 1], 1, 0)] + a + [pltpu.roll(a[0], 7, 0)]
            return v, [row[k] + row[k + 2] + 4.0 * s[k] for k in range(K)]

        def precondition(ge, w):
            eig6, inv_centre, stretch, inv_spread = coefficients(w)
            ic = full(inv_centre)

            def begin(i, c):
                for e in (2 * i, 2 * i + 1):
                    for k in range(K):
                        g = ge[w, e, pl.ds(k, 8, stride=K), :]
                        G[w, e, k] = g
                        U[0, w, e + 1, k] = g * ic
                return c

            lax.fori_loop(0, ER // 2, begin, 0)

            def sweep(n, ratio):
                p = n % 2
                ratio_next = 1.0 / (2.0 * stretch - ratio)
                momentum = ratio_next * ratio
                step = 2.0 * ratio_next * inv_spread
                cb, ce, c1 = full(step), full(step * eig6), full(1.0 + momentum)
                cp = full(jnp.where(n == 0, 0.0, momentum))
                clipped = (ER - HALO - n) // 2
                pairs = jnp.where(top | bottom, clipped, ER // 2 - 1 - n)
                low = jnp.where(top, HALO, jnp.where(bottom, ER - HALO - 2 * clipped, n + 1))

                def pair(i, c):
                    for e in (low + 2 * i, low + 2 * i + 1):
                        v, h = stencil(p, w, e + 1)
                        for k in range(K):
                            fresh = ce * (h[k] - KC[e, k] * v[k]) + cb * (G[w, e, k] - HC[e, k] * v[k])
                            fresh = fresh + (c1 * v[k] - cp * U[1 - p, w, e + 1, k])
                            U[1 - p, w, e + 1, k] = fresh * MK[k]
                    return c

                lax.fori_loop(0, pairs, pair, 0)
                return ratio_next

            lax.fori_loop(0, DEG - 1, sweep, 1.0 / stretch)

        def stencil_part(w, keep):
            eig6 = full(coefficients(w)[0])

            def one(i, c):
                for r in (2 * i, 2 * i + 1):
                    v, h = stencil((DEG - 1) % 2, w, r + HALO + 1)
                    for k in range(K):
                        keep[w, r, pl.ds(k, 8, stride=K), :] = v[k]
                        NQ[w, r, pl.ds(k, 8, stride=K), :] = eig6 * (KC[r + HALO, k] * v[k] - h[k])
                return c

            lax.fori_loop(0, ROWS // 2, one, 0)

        def pack(parts):
            out = jnp.zeros((8, LANES), jnp.float32)
            for at, part in enumerate(parts):
                out = jnp.where(sub8 == at, jnp.sum(part, axis=0, keepdims=True), out)
            return out

        def column_copy(at, i):
            return pltpu.make_async_remote_copy(
                src_ref=SA.at[at], dst_ref=RZ.at[at, z], send_sem=sum_send.at[at, 0],
                recv_sem=sum_recv.at[at, 0],
                device_id=(lax.rem(z + i, Z) * Y + y, d), device_id_type=MESH,
            )

        def plane_copy(at, i):
            return pltpu.make_async_remote_copy(
                src_ref=SG.at[at], dst_ref=RG.at[at, j], send_sem=sum_send.at[at, 1],
                recv_sem=sum_recv.at[at, 1],
                device_id=device(z, lax.rem(j + i, J)), device_id_type=MESH,
            )

        def wait_bytes(ref, count, sem):
            part = ref.at[pl.ds(0, count)]
            pltpu.make_async_copy(part, part, sem).wait()

        def column_start(at, value):
            SA[at] = value
            RZ[at, z] = value

            def one(i, c):
                column_copy(at, i).start()
                return c

            lax.fori_loop(1, Z, one, 0)

        def column_end(at):
            for side in (sum_recv, sum_send):
                wait_bytes(RZ.at[at], Z - 1, side.at[at, 0])
            return lax.fori_loop(1, Z, lambda i, c: c + RZ[at, i], RZ[at, 0])

        def plane_start(at, value):
            SG[at] = value
            RG[at, j] = value

            def one(i, c):
                plane_copy(at, i).start()
                return c

            lax.fori_loop(1, J, one, 0)

        def plane_end(at):
            for side in (sum_recv, sum_send):
                wait_bytes(RG.at[at], J - 1, side.at[at, 1])
            total = lax.fori_loop(1, J, lambda i, c: c + RG[at, i], RG[at, 0])
            return [jnp.sum(total[i : i + 1], axis=1, keepdims=True) for i in range(3)]

        zero = jnp.zeros((8, LANES), jnp.float32)

        def fold_cells(v):
            return jnp.sum(v.reshape(COLS // 8, 8, LANES), axis=0)

        def put_first(w, row, v):
            GE1[w, pl.ds(HALO + row, 2 * RB), OWN, :] = v

        def put_seen(w, row, v):
            NAT[w, pl.ds(row, 2 * RB)] = v

        all_wait(XR, 0)
        to_modes(lambda i: XR[i], put_first)
        for w in range(WIDE):
            halo_start(GE1, 0, w)
        send_tile(PS, XS, 1)
        for w in range(WIDE):
            halo_wait(GE1, 0, w)
            precondition(GE1, w)
            stencil_part(w, NZ)
        to_time(lambda w, rows: NZ[w, rows, OWN, :], TZ)
        all_wait(XS, 1)
        to_modes(lambda i: TZ[i] * XS[i], put_seen)

        sums = (zero, zero)
        for w in range(WIDE):
            def first_image(r, acc):
                fit, curve = acc
                zh = NZ[w, r, OWN, :]
                q = NQ[w, r, OWN, :] + NAT[w, r]
                GE2[w, r + HALO, OWN, :] = q
                return fit + fold_cells(GE1[w, r + HALO, OWN, :] * zh), curve + fold_cells(zh * q)

            sums = lax.fori_loop(0, ROWS, first_image, sums)
            halo_start(GE2, 1, w)
        column_start(0, pack(sums))
        send_days(TZ, FZ, 2)
        to_time(lambda w, rows: GE2[w, pl.ds(rows.start + HALO, rows.size), OWN, :], TQ)
        send_days(TQ, FQ, 3)

        for w in range(WIDE):
            halo_wait(GE2, 1, w)
            precondition(GE2, w)
            stencil_part(w, NW)
            if w == 0:
                plane_start(0, column_end(0))
        to_time(lambda w, rows: NW[w, rows, OWN, :], TW)
        send_days(TW, FW, 4)
        to_modes(lambda i: TW[i] * XS[i], put_seen)
        fit0, curve0, _ = plane_end(0)
        alpha0 = fit0 / curve0

        sums = (zero, zero, zero)
        for w in range(WIDE):
            def second_image(r, acc):
                fit, curve, cross = acc
                wh, g = NW[w, r, OWN, :], GE2[w, r + HALO, OWN, :]
                q = NQ[w, r, OWN, :] + NAT[w, r]
                NV[w, r] = q
                z1 = NZ[w, r, OWN, :] - alpha0 * wh
                r1 = GE1[w, r + HALO, OWN, :] - alpha0 * g
                return (
                    fit + fold_cells(r1 * z1), curve + fold_cells(z1 * (g - alpha0 * q)),
                    cross + fold_cells(z1 * g),
                )

            sums = lax.fori_loop(0, ROWS, second_image, sums)
        column_start(1, pack(sums))
        to_time(lambda w, rows: NV[w, rows], TV)
        send_days(TV, FV, 5)
        plane_start(1, column_end(1))
        fit1, curve1, cross1 = plane_end(1)
        beta = fit1 / fit0
        alpha1 = fit1 / (curve1 + 2.0 * beta * cross1 + beta * beta * curve0)
        c_old = alpha0 + alpha1 + alpha1 * beta
        c_new = alpha0 * alpha1

        def finish(part):
            def one(i, c):
                lanes = pl.ds(pl.multiple_of(i * LANES, LANES), LANES)
                values = []
                for q in range(4):
                    at = 4 * i + q
                    if part == 0:
                        values.append(c_old * FZ[at] - c_new * FW[at])
                    else:
                        values.append(PR[at] - c_old * FQ[at] + c_new * FV[at])
                for r, v in enumerate(swap(values)):
                    (sol, res)[part][r, :, lanes] = v
                return c

            lax.fori_loop(0, J // 4, one, 0)

        all_wait(FZ, 2)
        all_wait(FQ, 3)
        all_wait(FW, 4)
        finish(0)
        all_wait(FV, 5)
        finish(1)

        for at in range(6):
            all_wait_send(at)
        for q in range(4):
            @pl.when(4 * d + q != j)
            def _():
                cell_copy(q).wait_send()
        each_way(3, lambda at: near_copy(at).wait_send())
        for n, ge in enumerate((GE1, GE2)):
            for w in range(WIDE):
                each_way(3, lambda at: halo_copy(ge, n, w, at).wait_send())

    f32 = jnp.float32
    extended = pltpu.VMEM((WIDE, ER, EC, LANES), f32)
    strip = pltpu.VMEM((WIDE, ROWS, EC, LANES), f32)
    flat = pltpu.VMEM((WIDE, ROWS, COLS, LANES), f32)
    cell = pltpu.VMEM((ER, K, 8, LANES), f32)
    days = pltpu.VMEM((J, TB, LANES), f32)
    tile = pltpu.VMEM((Y, NT, LANES), f32)
    dma = pltpu.SemaphoreType.DMA
    scratch = [
        extended, extended, pltpu.VMEM((2, WIDE, ER + 2, K, 8, LANES), f32),
        pltpu.VMEM((WIDE, ER, K, 8, LANES), f32), cell, cell, pltpu.VMEM((2, ER, EC, LANES), f32),
        pltpu.VMEM((K, 8, LANES), f32), flat, strip, strip, strip, flat, days, days, tile, tile,
        tile, tile, tile, tile, days, days, days, days,
        pltpu.VMEM((4, 8, LANES), f32), pltpu.VMEM((Y, 8, LANES), f32),
        pltpu.VMEM((8, LANES), f32), pltpu.VMEM((8, 8, LANES), f32),
        pltpu.VMEM((2, 8, LANES), f32), pltpu.VMEM((2, Z, 8, LANES), f32),
        pltpu.VMEM((2, 8, LANES), f32), pltpu.VMEM((2, J, 8, LANES), f32),
        dma((2, WIDE, 8)), dma((2, WIDE, 8)), dma((8,)), dma((8,)), dma((6,)), dma((6,)),
        dma((4,)), dma((Y,)), dma((2, 2)), dma((2, 2)),
    ]
    return kernel, scratch


def solution(mesh):
    Z = mesh.shape["rows"] // Y
    D = mesh.shape["days"]
    kernel, scratch = make_kernel(Z, D)
    basis, modal = modal_constants(TB * D)
    vmem = pl.BlockSpec(memory_space=pltpu.VMEM)
    smem = pl.BlockSpec(memory_space=pltpu.SMEM)

    def body(observations, obs_mask, obs_weight, classes, kappa_table):
        shape = jax.ShapeDtypeStruct((RB, TB, COLS * Y * D), jnp.float32)
        sol, res = pl.pallas_call(
            kernel,
            out_shape=(shape, shape),
            in_specs=[vmem] * 4 + [smem] + [vmem] * 2,
            out_specs=(vmem, vmem),
            scratch_shapes=scratch,
            compiler_params=pltpu.CompilerParams(
                collective_id=0, has_side_effects=True, vmem_limit_bytes=48 * 1024 * 1024
            ),
        )(
            jnp.transpose(observations, (1, 0, 2)), jnp.transpose(obs_mask, (1, 0, 2)),
            obs_weight, classes, kappa_table, jnp.asarray(basis), jnp.asarray(modal),
        )
        return jnp.transpose(sol, (1, 0, 2)), jnp.transpose(res, (1, 0, 2))

    in_specs = (P("days", "rows", None), P("days", "rows", None), P("rows", None), P("rows", None), P())
    out_specs = (P("days", "rows", None), P("days", "rows", None))
    return jax.shard_map(body, mesh=mesh, in_specs=in_specs, out_specs=out_specs, check_vma=False)
```

time: 124 us -> 84 us (0.68)
  Pallas kernels: 118 us -> 78.5 us
    pallas_call x1, Pallas kernels: 118 us -> 78.5 us  [body(): pl.pallas_call(kernel, out_shape=(shape, shape), in_specs=[vmem] * 4 + [s...]
    unnamed x18 -> x16, local copies, waits for them, and re-layouts: 4.69 us -> 4.67 us
where the time goes in v2:
time: 84 us; the launch traced here: 83.9 us
  Pallas kernels  78.5 us (93%)
  local copies, waits for them, and re-layouts  4.67 us (6%)
    pallas_call x1, Pallas kernels, body(): pl.pallas_call(kernel, out_shape=(shape, shape), in_specs=[vmem] * 4 + [s...  78.5 us
    unnamed x16, local copies, waits for them, and re-layouts  4.67 us

profile of v2, /device:TPU:1, one launch (start us, length us, event | category | flops | bytes accessed | tf_op | source)
XLA Modules:
  0.0 83.9 jit_solution(2338785211243294519)
XLA Ops:
  0.6 0.0 copy-start.5
  0.6 1.4 %copy.16 = f32[32,4,1024]{2,0,1:T(8,128)S(1)} copy(f32[32,4,1024]{2,1,0:T(4,128)} %param.7) | data formatting | bytes 1048576 | tf_op args[0]
  2.0 0.0 copy-done.5
  2.1 0.0 copy-start
  2.1 0.0 copy-start.1
  2.1 0.0 copy-start.2
  2.1 0.0 copy-start.3
  2.1 0.3 copy.15
  2.4 0.0 copy-start.4
  2.4 0.6 copy-done
  3.0 0.0 copy-done.1
  3.0 0.0 copy-done.2
  3.0 0.0 copy-done.3
  3.0 0.1 copy-done.4
  3.1 78.5 %shard_map.86 = (f32[4,32,1024]{2,1,0:T(8,128)S(1)}, f32[4,32,1024]{2,1,0:T(8,128)S(1)}) custom-call(f32[4,32,1024]{2,1,0:T(8,128)S(1)} %bitcast.8, s32[4,32,1024]{2,1,0:T(8,128)S(1)} %bitcast.9, f32[4,1024]{1,0:T(4,128)S(1)} %copy-done.1, s32[4,1024]{1,0:T(4,128)S(1)} %copy-done.2, f32[16]{0:T(128)S(1)} %copy-done.4, f32[256,256]{1,0:T(8,128)S(1)} %copy-done, ...), custom_call_target="tpu_custom_call" | custom-call | tf_op jit(solution)/shard_map/pallas_call | solution.py:598
  81.6 1.1 %copy.11 = f32[32,4,1024]{2,1,0:T(4,128)} copy(f32[32,4,1024]{2,0,1:T(8,128)S(1)} %bitcast.11) | data formatting | bytes 1048576
  82.8 1.1 %copy.12 = f32[32,4,1024]{2,1,0:T(4,128)} copy(f32[32,4,1024]{2,0,1:T(8,128)S(1)} %bitcast.10) | data formatting | bytes 1048576
Async XLA Ops:
  0.6 1.4 %copy-start.5 = (s32[32,4,1024]{2,1,0:T(4,128)S(1)}, s32[32,4,1024]{2,1,0:T(4,128)}, u32[]{:S(2)}) copy-start(s32[32,4,1024]{2,1,0:T(4,128)} %param.8) | copy-start | bytes 1572868
  2.1 1.0 %copy-start = (f32[256,256]{1,0:T(8,128)S(1)}, f32[256,256]{1,0:T(8,128)}, u32[]{:S(2)}) copy-start(f32[256,256]{1,0:T(8,128)} %constant.4.clone.basis) | copy-start | bytes 786436
  2.1 0.9 %copy-start.1 = (f32[4,1024]{1,0:T(4,128)S(1)}, f32[4,1024]{1,0:T(4,128)}, u32[]{:S(2)}) copy-start(f32[4,1024]{1,0:T(4,128)} %weight.1) | copy-start | bytes 49156
  2.1 0.9 %copy-start.2 = (s32[4,1024]{1,0:T(4,128)S(1)}, s32[4,1024]{1,0:T(4,128)}, u32[]{:S(2)}) copy-start(s32[4,1024]{1,0:T(4,128)} %classes.1) | copy-start | bytes 49156
  2.1 0.9 %copy-start.3 = (f32[8,256]{1,0:T(8,128)S(1)}, f32[8,256]{1,0:T(8,128)}, u32[]{:S(2)}) copy-start(f32[8,256]{1,0:T(8,128)} %constant.5.clone.modal) | copy-start | bytes 24580
  2.4 0.7 copy-start.4

commit v3 on v2

--- a/solution.py
+++ b/solution.py
@@ -26,6 +26,7 @@
 HALO = 8
 K = (COLS + 2 * HALO) // 8
 LANES = 128
+GROUP = 4
 
 
 def modal_constants(total):
@@ -37,7 +38,9 @@
     upper = eig * (KAPPA_HIGH + STENCIL_TOP) + HALF_OBS * WEIGHT_HIGH
     centre, spread = 0.5 * (upper + lower), 0.5 * (upper - lower)
     rows = np.zeros((8, total), np.float32)
-    for at, row in enumerate((eig / STENCIL_SCALE, 1.0 / centre, centre / spread, 1.0 / spread)):
+    for at, row in enumerate(
+        (eig / STENCIL_SCALE, 1.0 / centre, centre / spread, 1.0 / spread, STENCIL_SCALE / eig)
+    ):
         rows[at] = row
     return basis.astype(np.float32), rows
 
@@ -47,24 +50,27 @@
     ROWS = RB * Y
     J = Y * D
     WIDE = NT // LANES
+    DBITS = D.bit_length() - 1
+    SLABS = J // 4
     ER, EC = ROWS + 2 * HALO, COLS + 2 * HALO
     OWN = pl.ds(HALO, COLS)
 
     def kernel(
-        obs, mask, weight, classes, kappa, basis, modal, sol, res,
-        GE1, GE2, U, G, KC, HC, NC, MK, NAT, NQ, NZ, NW, NV, PR, PS, XR, XS,
+        obs_in, mask_in, weight_in, classes_in, kappa, basis_in, modal_in, sol, res,
+        obs, mask, weight, classes, basis, modal,
+        GE1, GE2, U, DX, G, KC, SC, NC, MK, NAT, NQ, NZ, NW, NV, PR, PS, XR, XS,
         TZ, TQ, TW, TV, FZ, FQ, FW, FV, PW, CW, CT, CN, SA, RZ, SG, RG,
         halo_send, halo_recv, near_send, near_recv, all_send, all_recv, cell_send, cell_recv,
-        sum_send, sum_recv,
+        sum_send, sum_recv, load_sem,
     ):
         ri, d = lax.axis_index("rows"), lax.axis_index("days")
         z, y = ri // Y, ri % Y
-        j = y * D + jnp.where(y % 2 == 0, d, D - 1 - d)
+        j = y * D + (d ^ ((D - 1) * (y & 1)))
         top, bottom, left, right = z == 0, z == Z - 1, j == 0, j == J - 1
 
         def place(jt):
-            yt, mt = jt // D, jt % D
-            return yt, jnp.where(yt % 2 == 0, mt, D - 1 - mt)
+            yt = jt >> DBITS
+            return yt, (jt & (D - 1)) ^ ((D - 1) * (yt & 1))
 
         def device(zt, jt):
             yt, dt = place(jt)
@@ -74,17 +80,15 @@
         west, east = lax.rem(j + J - 1, J), lax.rem(j + 1, J)
 
         CN[...] = jnp.zeros_like(CN)
-        for cond, rows, cols in (
-            (top, pl.ds(0, HALO), pl.ds(0, EC)),
-            (bottom, pl.ds(HALO + ROWS, HALO), pl.ds(0, EC)),
-            (left, pl.ds(0, ER), pl.ds(0, HALO)),
-            (right, pl.ds(0, ER), pl.ds(HALO + COLS, HALO)),
-        ):
-            @pl.when(cond)
-            def _():
-                for ge in (GE1, GE2):
-                    for w in range(WIDE):
-                        ge[w, rows, cols, :] = jnp.zeros((rows.size, cols.size, LANES), jnp.float32)
+        loads = [
+            pltpu.make_async_copy(src, dst, load_sem.at[i])
+            for i, (src, dst) in enumerate((
+                (weight_in, weight), (classes_in, classes), (obs_in, obs), (mask_in, mask),
+                (basis_in, basis), (modal_in, modal),
+            ))
+        ]
+        for load in loads:
+            load.start()
 
         barrier = pltpu.get_barrier_semaphore()
 
@@ -92,11 +96,11 @@
             pl.semaphore_signal(barrier, inc=1, device_id=target, device_id_type=MESH)
 
         def greet_plane(i, c):
-            greet(device(z, lax.rem(j + i, J)))
+            greet(device(z, ((j + i) & (J - 1))))
             return c
 
         def greet_column(i, c):
-            greet((lax.rem(z + i, Z) * Y + y, d))
+            greet((((z + i) & (Z - 1)) * Y + y, d))
             return c
 
         lax.fori_loop(1, J, greet_plane, 0)
@@ -104,6 +108,9 @@
         for zt in (north, south):
             for jt in (west, east):
                 greet(device(zt, jt))
+
+        def full(v):
+            return jnp.broadcast_to(v, (8, LANES))
 
         def swap(parts):
             lane = lax.broadcasted_iota(jnp.int32, parts[0].shape, 1)
@@ -118,6 +125,8 @@
             d3 = jnp.where(even, pltpu.roll(t2, 96, 1), t3)
             return d0, d1, d2, d3
 
+        loads[0].wait()
+        loads[1].wait()
         slab = pl.ds(pl.multiple_of(d * LANES, LANES), LANES)
         cls = classes[:, slab]
         kap = jnp.zeros((RB, LANES), jnp.float32)
@@ -133,22 +142,6 @@
         for q, part in enumerate(swap(cells)):
             PW[q] = part
 
-        def shuffle_seen(i, c):
-            lanes = pl.ds(pl.multiple_of(i * LANES, LANES), LANES)
-            seen, rhs = [], []
-            for r in range(RB):
-                s = mask[r, :, lanes].astype(jnp.float32) * weight[r : r + 1, lanes]
-                seen.append(s)
-                rhs.append(s * obs[r, :, lanes])
-            for q, part in enumerate(swap(rhs)):
-                PR[4 * i + q] = part
-            for q, part in enumerate(swap(seen)):
-                PS[4 * i + q] = part
-            return c
-
-        lax.fori_loop(0, J // 4, shuffle_seen, 0)
-        U[...] = jnp.zeros_like(U)
-
         pl.semaphore_wait(barrier, (J - 1) + (Z - 1) + 4)
 
         def cell_copy(q):
@@ -170,7 +163,7 @@
                 cell_local(q).start()
 
         def to_tile(src, dst, at, i):
-            jt = lax.rem(j + i, J)
+            jt = ((j + i) & (J - 1))
             return pltpu.make_async_remote_copy(
                 src_ref=src.at[jt], dst_ref=dst.at[y, pl.ds(pl.multiple_of(d * TB, TB), TB)],
                 send_sem=all_send.at[at], recv_sem=all_recv.at[at],
@@ -178,7 +171,7 @@
             )
 
         def to_days(src, dst, at, i):
-            jt = lax.rem(j + i, J)
+            jt = ((j + i) & (J - 1))
             yt, dt = place(jt)
             return pltpu.make_async_remote_copy(
                 src_ref=src.at[yt, pl.ds(pl.multiple_of(dt * TB, TB), TB)], dst_ref=dst.at[j],
@@ -186,24 +179,30 @@
                 device_id=device(z, jt), device_id_type=MESH,
             )
 
-        def send_all(copy, src, dst, at):
+        def send_range(copy, src, dst, at, low, high):
             def one(i, c):
                 copy(src, dst, at, i).start()
                 return c
 
-            lax.fori_loop(1, J, one, 0)
-
-        def send_tile(src, dst, at):
-            send_all(to_tile, src, dst, at)
+            lax.fori_loop(low, high, one, 0)
+
+        def own_tile(src, dst, at):
             pltpu.make_async_copy(
                 src.at[j], dst.at[y, pl.ds(pl.multiple_of(d * TB, TB), TB)], all_recv.at[at]
             ).start()
 
-        def send_days(src, dst, at):
-            send_all(to_days, src, dst, at)
+        def own_days(src, dst, at):
             pltpu.make_async_copy(
                 src.at[y, pl.ds(pl.multiple_of(d * TB, TB), TB)], dst.at[j], all_recv.at[at]
             ).start()
+
+        def send_tile(src, dst, at):
+            send_range(to_tile, src, dst, at, 1, J)
+            own_tile(src, dst, at)
+
+        def send_days(src, dst, at):
+            send_range(to_days, src, dst, at, 1, J)
+            own_days(src, dst, at)
 
         def all_wait(dst, at):
             pltpu.make_async_copy(dst, dst, all_recv.at[at]).wait()
@@ -259,7 +258,55 @@
         def halo_wait(ge, n, w):
             each_way(4, lambda at: halo_copy(ge, n, w, at).wait_recv())
 
-        send_tile(PR, XR, 0)
+        def day_rows(i, r, t):
+            return pl.ds(t * SLABS * RB + RB * i + r, 8, stride=SLABS * RB)
+
+        def seen_rows(i, r):
+            lanes = pl.ds(pl.multiple_of(i * LANES, LANES), LANES)
+            seen = [mask[day_rows(i, r, t), :] for t in range(0, TB, 8)]
+            return jnp.concatenate(seen, axis=0).astype(jnp.float32) * weight[r : r + 1, lanes]
+
+        for load in loads[2:]:
+            load.wait()
+
+        def shuffle_rhs(step, c):
+            i = ((j >> 2) + step) & (SLABS - 1)
+            rhs = []
+            for r in range(RB):
+                seen = [obs[day_rows(i, r, t), :] for t in range(0, TB, 8)]
+                rhs.append(seen_rows(i, r) * jnp.concatenate(seen, axis=0))
+            for q, part in enumerate(swap(rhs)):
+                PR[4 * i + q] = part
+            for q in range(4):
+                @pl.when(4 * i + q != j)
+                def _():
+                    to_tile(PR, XR, 0, 4 * i + q - j).start()
+
+            return c
+
+        lax.fori_loop(0, SLABS, shuffle_rhs, 0)
+        own_tile(PR, XR, 0)
+
+        def shuffle_seen(i, c):
+            for q, part in enumerate(swap([seen_rows(i, r) for r in range(RB)])):
+                PS[4 * i + q] = part
+            return c
+
+        lax.fori_loop(0, SLABS, shuffle_seen, 0)
+
+        for cond, rows, cols in (
+            (top, pl.ds(0, HALO), pl.ds(0, EC)),
+            (bottom, pl.ds(HALO + ROWS, HALO), pl.ds(0, EC)),
+            (left, pl.ds(0, ER), pl.ds(0, HALO)),
+            (right, pl.ds(0, ER), pl.ds(HALO + COLS, HALO)),
+        ):
+            @pl.when(cond)
+            def _():
+                for ge in (GE1, GE2):
+                    for w in range(WIDE):
+                        ge[w, rows, cols, :] = jnp.zeros((rows.size, cols.size, LANES), jnp.float32)
+
+        U[...] = jnp.zeros_like(U)
 
         for yt in range(Y):
             pltpu.make_async_copy(CW.at[yt], CW.at[yt], cell_recv.at[yt]).wait()
@@ -276,7 +323,7 @@
             MK[k] = jnp.where(outside, 0.0, 1.0)
 
         def spread_tile(source, dz, dj):
-            for f, scale, shift in ((0, HALF_OBS, 0.0), (1, STENCIL_SCALE, 20.0)):
+            for f, scale, shift in ((0, HALF_OBS, 0.0), (1, STENCIL_SCALE, 36.0)):
                 for yt in range(Y):
                     if (dz < 0 and RB * (yt + 1) <= ROWS - HALO) or (dz > 0 and RB * yt >= HALO):
                         continue
@@ -296,10 +343,15 @@
         for at, way in enumerate(ways):
             spread_tile(CN[at], -way[0], -way[1])
 
+        inv_eig = [full(modal[4:5, w * LANES : (w + 1) * LANES]) for w in range(WIDE)]
+
         def interleave_cells(e, c):
             for k in range(K):
-                HC[e, k] = NC[0, e, pl.ds(k, 8, stride=K), :]
-                KC[e, k] = NC[1, e, pl.ds(k, 8, stride=K), :]
+                hc = NC[0, e, pl.ds(k, 8, stride=K), :]
+                kc = NC[1, e, pl.ds(k, 8, stride=K), :]
+                KC[e, k] = kc
+                for w in range(WIDE):
+                    SC[w, e, k] = hc * inv_eig[w] + kc
             return c
 
         lax.fori_loop(0, ER, interleave_cells, 0)
@@ -330,30 +382,32 @@
 
             lax.fori_loop(0, Y // 2, one, 0)
 
-        def full(v):
-            return jnp.broadcast_to(v, (8, LANES))
-
         def coefficients(w):
             lanes = slice(w * LANES, (w + 1) * LANES)
             return [modal[i : i + 1, lanes] for i in range(4)]
 
-        def stencil(p, w, u):
-            v = [U[p, w, u, k] for k in range(K)]
-            s = [U[p, w, u - 1, k] + U[p, w, u + 1, k] for k in range(K)]
-            a = [4.0 * v[k] + s[k] for k in range(K)]
-            row = [pltpu.roll(a[K - 1], 1, 0)] + a + [pltpu.roll(a[0], 7, 0)]
-            return v, [row[k] + row[k + 2] + 4.0 * s[k] for k in range(K)]
+        def rows_of(p, w, first, count):
+            above = [U[p, w, first, k] for k in range(K)]
+            here = [U[p, w, first + 1, k] for k in range(K)]
+            for i in range(count):
+                below = [U[p, w, first + 2 + i, k] for k in range(K)]
+                b = [4.0 * here[k] + (above[k] + below[k]) for k in range(K)]
+                line = [pltpu.roll(b[K - 1], 1, 0)] + b + [pltpu.roll(b[0], 7, 0)]
+                yield i, here, [(line[k] + line[k + 2]) + 4.0 * b[k] for k in range(K)]
+                above, here = here, below
 
         def precondition(ge, w):
             eig6, inv_centre, stretch, inv_spread = coefficients(w)
-            ic = full(inv_centre)
+            ic, ie = full(inv_centre), inv_eig[w]
 
             def begin(i, c):
                 for e in (2 * i, 2 * i + 1):
                     for k in range(K):
                         g = ge[w, e, pl.ds(k, 8, stride=K), :]
-                        G[w, e, k] = g
-                        U[0, w, e + 1, k] = g * ic
+                        G[w, e, k] = g * ie
+                        u = g * ic
+                        U[0, w, e + 1, k] = u
+                        DX[w, e, k] = u
                 return c
 
             lax.fori_loop(0, ER // 2, begin, 0)
@@ -361,24 +415,25 @@
             def sweep(n, ratio):
                 p = n % 2
                 ratio_next = 1.0 / (2.0 * stretch - ratio)
-                momentum = ratio_next * ratio
-                step = 2.0 * ratio_next * inv_spread
-                cb, ce, c1 = full(step), full(step * eig6), full(1.0 + momentum)
-                cp = full(jnp.where(n == 0, 0.0, momentum))
-                clipped = (ER - HALO - n) // 2
-                pairs = jnp.where(top | bottom, clipped, ER // 2 - 1 - n)
-                low = jnp.where(top, HALO, jnp.where(bottom, ER - HALO - 2 * clipped, n + 1))
-
-                def pair(i, c):
-                    for e in (low + 2 * i, low + 2 * i + 1):
-                        v, h = stencil(p, w, e + 1)
+                momentum = full(ratio_next * ratio)
+                step = full(2.0 * ratio_next * inv_spread * eig6)
+                clipped = (ER - HALO + GROUP - 2 - n) // GROUP
+                groups = jnp.where(top | bottom, clipped, (ER + GROUP - 3 - 2 * n) // GROUP)
+                low = jnp.where(bottom, ER - HALO - GROUP * groups, ER // 2 - GROUP // 2 * groups)
+                low = jnp.where(top, HALO, low)
+
+                def group(i, c):
+                    first = low + GROUP * i
+                    for at, v, h in rows_of(p, w, first, GROUP):
+                        e = first + at
                         for k in range(K):
-                            fresh = ce * (h[k] - KC[e, k] * v[k]) + cb * (G[w, e, k] - HC[e, k] * v[k])
-                            fresh = fresh + (c1 * v[k] - cp * U[1 - p, w, e + 1, k])
-                            U[1 - p, w, e + 1, k] = fresh * MK[k]
+                            dx = step * ((G[w, e, k] - SC[w, e, k] * v[k]) + h[k])
+                            dx = (momentum * DX[w, e, k] + dx) * MK[k]
+                            DX[w, e, k] = dx
+                            U[1 - p, w, e + 1, k] = v[k] + dx
                     return c
 
-                lax.fori_loop(0, pairs, pair, 0)
+                lax.fori_loop(0, groups, group, 0)
                 return ratio_next
 
             lax.fori_loop(0, DEG - 1, sweep, 1.0 / stretch)
@@ -387,14 +442,15 @@
             eig6 = full(coefficients(w)[0])
 
             def one(i, c):
-                for r in (2 * i, 2 * i + 1):
-                    v, h = stencil((DEG - 1) % 2, w, r + HALO + 1)
+                first = GROUP * i
+                for at, v, h in rows_of((DEG - 1) % 2, w, first + HALO, GROUP):
+                    r = first + at
                     for k in range(K):
                         keep[w, r, pl.ds(k, 8, stride=K), :] = v[k]
                         NQ[w, r, pl.ds(k, 8, stride=K), :] = eig6 * (KC[r + HALO, k] * v[k] - h[k])
                 return c
 
-            lax.fori_loop(0, ROWS // 2, one, 0)
+            lax.fori_loop(0, ROWS // GROUP, one, 0)
 
         def pack(parts):
             out = jnp.zeros((8, LANES), jnp.float32)
@@ -406,14 +462,14 @@
             return pltpu.make_async_remote_copy(
                 src_ref=SA.at[at], dst_ref=RZ.at[at, z], send_sem=sum_send.at[at, 0],
                 recv_sem=sum_recv.at[at, 0],
-                device_id=(lax.rem(z + i, Z) * Y + y, d), device_id_type=MESH,
+                device_id=(((z + i) & (Z - 1)) * Y + y, d), device_id_type=MESH,
             )
 
         def plane_copy(at, i):
             return pltpu.make_async_remote_copy(
                 src_ref=SG.at[at], dst_ref=RG.at[at, j], send_sem=sum_send.at[at, 1],
                 recv_sem=sum_recv.at[at, 1],
-                device_id=device(z, lax.rem(j + i, J)), device_id_type=MESH,
+                device_id=device(z, ((j + i) & (J - 1))), device_id_type=MESH,
             )
 
         def wait_bytes(ref, count, sem):
@@ -520,8 +576,10 @@
             sums = lax.fori_loop(0, ROWS, second_image, sums)
         column_start(1, pack(sums))
         to_time(lambda w, rows: NV[w, rows], TV)
-        send_days(TV, FV, 5)
+        own_days(TV, FV, 5)
+        send_range(to_days, TV, FV, 5, 1, 12)
         plane_start(1, column_end(1))
+        send_range(to_days, TV, FV, 5, 12, J)
         fit1, curve1, cross1 = plane_end(1)
         beta = fit1 / fit0
         alpha1 = fit1 / (curve1 + 2.0 * beta * cross1 + beta * beta * curve0)
@@ -530,7 +588,6 @@
 
         def finish(part):
             def one(i, c):
-                lanes = pl.ds(pl.multiple_of(i * LANES, LANES), LANES)
                 values = []
                 for q in range(4):
                     at = 4 * i + q
@@ -539,15 +596,16 @@
                     else:
                         values.append(PR[at] - c_old * FQ[at] + c_new * FV[at])
                 for r, v in enumerate(swap(values)):
-                    (sol, res)[part][r, :, lanes] = v
-                return c
-
-            lax.fori_loop(0, J // 4, one, 0)
+                    for t in range(0, TB, 8):
+                        (sol, res)[part][day_rows(i, r, t), :] = v[t : t + 8]
+                return c
+
+            lax.fori_loop(0, SLABS, one, 0)
 
         all_wait(FZ, 2)
-        all_wait(FQ, 3)
         all_wait(FW, 4)
         finish(0)
+        all_wait(FQ, 3)
         all_wait(FV, 5)
         finish(1)
 
@@ -566,13 +624,17 @@
     extended = pltpu.VMEM((WIDE, ER, EC, LANES), f32)
     strip = pltpu.VMEM((WIDE, ROWS, EC, LANES), f32)
     flat = pltpu.VMEM((WIDE, ROWS, COLS, LANES), f32)
+    fields = pltpu.VMEM((WIDE, ER, K, 8, LANES), f32)
     cell = pltpu.VMEM((ER, K, 8, LANES), f32)
     days = pltpu.VMEM((J, TB, LANES), f32)
     tile = pltpu.VMEM((Y, NT, LANES), f32)
     dma = pltpu.SemaphoreType.DMA
+    given = pltpu.VMEM((TB * SLABS * RB, LANES), f32)
     scratch = [
+        given, pltpu.VMEM((TB * SLABS * RB, LANES), jnp.int32), pltpu.VMEM((RB, J * COLS), f32),
+        pltpu.VMEM((RB, J * COLS), jnp.int32), pltpu.VMEM((NT, NT), f32), pltpu.VMEM((8, NT), f32),
         extended, extended, pltpu.VMEM((2, WIDE, ER + 2, K, 8, LANES), f32),
-        pltpu.VMEM((WIDE, ER, K, 8, LANES), f32), cell, cell, pltpu.VMEM((2, ER, EC, LANES), f32),
+        fields, fields, cell, fields, pltpu.VMEM((2, ER, EC, LANES), f32),
         pltpu.VMEM((K, 8, LANES), f32), flat, strip, strip, strip, flat, days, days, tile, tile,
         tile, tile, tile, tile, days, days, days, days,
         pltpu.VMEM((4, 8, LANES), f32), pltpu.VMEM((Y, 8, LANES), f32),
@@ -580,7 +642,7 @@
         pltpu.VMEM((2, 8, LANES), f32), pltpu.VMEM((2, Z, 8, LANES), f32),
         pltpu.VMEM((2, 8, LANES), f32), pltpu.VMEM((2, J, 8, LANES), f32),
         dma((2, WIDE, 8)), dma((2, WIDE, 8)), dma((8,)), dma((8,)), dma((6,)), dma((6,)),
-        dma((4,)), dma((Y,)), dma((2, 2)), dma((2, 2)),
+        dma((4,)), dma((Y,)), dma((2, 2)), dma((2, 2)), dma((6,)),
     ]
     return kernel, scratch
 
@@ -590,25 +652,35 @@
     D = mesh.shape["days"]
     kernel, scratch = make_kernel(Z, D)
     basis, modal = modal_constants(TB * D)
+    slabs = Y * D // 4
     vmem = pl.BlockSpec(memory_space=pltpu.VMEM)
     smem = pl.BlockSpec(memory_space=pltpu.SMEM)
+    hbm = pl.BlockSpec(memory_space=pl.ANY)
+
+    def by_slab(array):
+        array = array.reshape(TB, RB, slabs, LANES)
+        return jnp.transpose(array, (0, 2, 1, 3)).reshape(TB * slabs * RB, LANES)
+
+    def by_row(array):
+        array = array.reshape(TB, slabs, RB, LANES)
+        return jnp.transpose(array, (0, 2, 1, 3)).reshape(TB, RB, slabs * LANES)
 
     def body(observations, obs_mask, obs_weight, classes, kappa_table):
-        shape = jax.ShapeDtypeStruct((RB, TB, COLS * Y * D), jnp.float32)
+        shape = jax.ShapeDtypeStruct((TB * slabs * RB, LANES), jnp.float32)
         sol, res = pl.pallas_call(
             kernel,
             out_shape=(shape, shape),
-            in_specs=[vmem] * 4 + [smem] + [vmem] * 2,
+            in_specs=[hbm] * 4 + [smem] + [hbm] * 2,
             out_specs=(vmem, vmem),
             scratch_shapes=scratch,
             compiler_params=pltpu.CompilerParams(
-                collective_id=0, has_side_effects=True, vmem_limit_bytes=48 * 1024 * 1024
+                collective_id=0, has_side_effects=True, vmem_limit_bytes=56 * 1024 * 1024
             ),
         )(
-            jnp.transpose(observations, (1, 0, 2)), jnp.transpose(obs_mask, (1, 0, 2)),
-            obs_weight, classes, kappa_table, jnp.asarray(basis), jnp.asarray(modal),
+            by_slab(observations), by_slab(obs_mask), obs_weight, classes, kappa_table,
+            jnp.asarray(basis), jnp.asarray(modal),
         )
-        return jnp.transpose(sol, (1, 0, 2)), jnp.transpose(res, (1, 0, 2))
+        return by_row(sol), by_row(res)
 
     in_specs = (P("days", "rows", None), P("days", "rows", None), P("rows", None), P("rows", None), P())
     out_specs = (P("days", "rows", None), P("days", "rows", None))

time: 84 us -> 81.4 us (0.969)
  local copies, waits for them, and re-layouts: 4.67 us -> 2.72 us
  Pallas kernels: 78.5 us -> 77.5 us
    unnamed x16 -> x4, local copies, waits for them, and re-layouts: 4.67 us -> 2.72 us
    pallas_call x1, Pallas kernels: 78.5 us -> 77.5 us  [body(): pl.pallas_call(kernel, out_shape=(shape, shape), in_specs=[hbm] * 4 + [sm...]
where the time goes in v3:
time: 81.4 us; the launch traced here: 80.9 us
  Pallas kernels  77.5 us (95%)
  local copies, waits for them, and re-layouts  2.72 us (3%)
    pallas_call x1, Pallas kernels, body(): pl.pallas_call(kernel, out_shape=(shape, shape), in_specs=[hbm] * 4 + [sm...  77.5 us
    unnamed x4, local copies, waits for them, and re-layouts  2.72 us

profile of v3, /device:TPU:1, one launch (start us, length us, event | category | flops | bytes accessed | tf_op | source)
XLA Modules:
  0.0 80.9 jit_solution(16900895927956841973)
XLA Ops:
  0.6 77.5 %shard_map.86 = (f32[1024,128]{1,0:T(8,128)}, f32[1024,128]{1,0:T(8,128)}) custom-call(f32[1024,128]{1,0:T(8,128)} %bitcast.20, s32[1024,128]{1,0:T(8,128)} %bitcast.21, f32[4,1024]{1,0:T(4,128)} %weight_in.1, s32[4,1024]{1,0:T(4,128)} %classes_in.1, f32[16]{0:T(128)} %kappa.1, f32[256,256]{1,0:T(8,128)} %constant.4.clone.basis_in, ...), custom_call_target="tpu_custom_call" | custom-call | tf_op jit(solution)/shard_map/pallas_call | solution.py:670
  78.2 0.0 copy-start
  78.2 1.9 %copy.15 = f32[32,4,1024]{2,1,0:T(4,128)} copy(f32[32,4,1024]{2,1,0:T(4,128)} %bitcast.23) | data formatting | bytes 1048576
  80.1 0.0 copy-done
  80.1 0.8 copy.16
Async XLA Ops:
  78.2 1.9 %copy-start = (f32[1024,128]{1,0:T(8,128)S(1)}, f32[1024,128]{1,0:T(8,128)}, u32[]{:S(2)}) copy-start(f32[1024,128]{1,0:T(8,128)} %get-tuple-element.5) | copy-start | bytes 1572868

commit v4 on v3

--- a/solution.py
+++ b/solution.py
@@ -59,9 +59,9 @@
         obs_in, mask_in, weight_in, classes_in, kappa, basis_in, modal_in, sol, res,
         obs, mask, weight, classes, basis, modal,
         GE1, GE2, U, DX, G, KC, SC, NC, MK, NAT, NQ, NZ, NW, NV, PR, PS, XR, XS,
-        TZ, TQ, TW, TV, FZ, FQ, FW, FV, PW, CW, CT, CN, SA, RZ, SG, RG,
+        TZ, TQ, TW, TV, FZ, FQ, FW, FV, PW, CW, CT, CN, SA, RS, sol_out, res_out,
         halo_send, halo_recv, near_send, near_recv, all_send, all_recv, cell_send, cell_recv,
-        sum_send, sum_recv, load_sem,
+        sum_send, sum_recv, load_sem, out_sem,
     ):
         ri, d = lax.axis_index("rows"), lax.axis_index("days")
         z, y = ri // Y, ri % Y
@@ -142,6 +142,28 @@
         for q, part in enumerate(swap(cells)):
             PW[q] = part
 
+        def day_rows(i, r, t):
+            return pl.ds(t * SLABS * RB + RB * i + r, 8, stride=SLABS * RB)
+
+        def seen_rows(i, r):
+            lanes = pl.ds(pl.multiple_of(i * LANES, LANES), LANES)
+            seen = [mask[day_rows(i, r, t), :] for t in range(0, TB, 8)]
+            return jnp.concatenate(seen, axis=0).astype(jnp.float32) * weight[r : r + 1, lanes]
+
+        for load in loads[2:]:
+            load.wait()
+
+        def shuffle_rhs(i, c):
+            rhs = []
+            for r in range(RB):
+                seen = [obs[day_rows(i, r, t), :] for t in range(0, TB, 8)]
+                rhs.append(seen_rows(i, r) * jnp.concatenate(seen, axis=0))
+            for q, part in enumerate(swap(rhs)):
+                PR[4 * i + q] = part
+            return c
+
+        lax.fori_loop(0, SLABS, shuffle_rhs, 0)
+
         pl.semaphore_wait(barrier, (J - 1) + (Z - 1) + 4)
 
         def cell_copy(q):
@@ -212,6 +234,7 @@
                 PR.at[pl.ds(0, J - 1)], PR.at[pl.ds(0, J - 1)], all_send.at[at]
             ).wait()
 
+        SIDES, ENDS = (2, 3), (0, 1, 4, 5, 6, 7)
         ways = []
         for dz, dj in ((-1, 0), (1, 0), (0, -1), (0, 1), (-1, -1), (-1, 1), (1, -1), (1, 1)):
             to_ok, from_ok = True, True
@@ -246,8 +269,10 @@
                 device_id=target, device_id_type=MESH,
             )
 
-        def each_way(which, do):
-            for at, way in enumerate(ways):
+        def each_way(which, do, among=range(8)):
+            for at in among:
+                way = ways[at]
+
                 @pl.when(way[which])
                 def _():
                     do(at)
@@ -255,36 +280,14 @@
         def halo_start(ge, n, w):
             each_way(3, lambda at: halo_copy(ge, n, w, at).start())
 
-        def halo_wait(ge, n, w):
-            each_way(4, lambda at: halo_copy(ge, n, w, at).wait_recv())
-
-        def day_rows(i, r, t):
-            return pl.ds(t * SLABS * RB + RB * i + r, 8, stride=SLABS * RB)
-
-        def seen_rows(i, r):
-            lanes = pl.ds(pl.multiple_of(i * LANES, LANES), LANES)
-            seen = [mask[day_rows(i, r, t), :] for t in range(0, TB, 8)]
-            return jnp.concatenate(seen, axis=0).astype(jnp.float32) * weight[r : r + 1, lanes]
-
-        for load in loads[2:]:
-            load.wait()
-
-        def shuffle_rhs(step, c):
-            i = ((j >> 2) + step) & (SLABS - 1)
-            rhs = []
-            for r in range(RB):
-                seen = [obs[day_rows(i, r, t), :] for t in range(0, TB, 8)]
-                rhs.append(seen_rows(i, r) * jnp.concatenate(seen, axis=0))
-            for q, part in enumerate(swap(rhs)):
-                PR[4 * i + q] = part
-            for q in range(4):
-                @pl.when(4 * i + q != j)
-                def _():
-                    to_tile(PR, XR, 0, 4 * i + q - j).start()
-
+        def halo_wait(ge, n, w, among):
+            each_way(4, lambda at: halo_copy(ge, n, w, at).wait_recv(), among)
+
+        def send_rhs(i, c):
+            to_tile(PR, XR, 0, i).start()
             return c
 
-        lax.fori_loop(0, SLABS, shuffle_rhs, 0)
+        lax.fori_loop(1, J, send_rhs, 0)
         own_tile(PR, XR, 0)
 
         def shuffle_seen(i, c):
@@ -306,7 +309,6 @@
                     for w in range(WIDE):
                         ge[w, rows, cols, :] = jnp.zeros((rows.size, cols.size, LANES), jnp.float32)
 
-        U[...] = jnp.zeros_like(U)
 
         for yt in range(Y):
             pltpu.make_async_copy(CW.at[yt], CW.at[yt], cell_recv.at[yt]).wait()
@@ -320,7 +322,8 @@
         column = lax.broadcasted_iota(jnp.int32, (8, LANES), 0) * K
         for k in range(K):
             outside = (left & (column + k < HALO)) | (right & (column + k >= HALO + COLS))
-            MK[k] = jnp.where(outside, 0.0, 1.0)
+            MK[0, k] = jnp.zeros((8, LANES), jnp.float32)
+            MK[1, k] = jnp.where(outside, 0.0, 1.0)
 
         def spread_tile(source, dz, dj):
             for f, scale, shift in ((0, HALF_OBS, 0.0), (1, STENCIL_SCALE, 36.0)):
@@ -387,58 +390,96 @@
             return [modal[i : i + 1, lanes] for i in range(4)]
 
         def rows_of(p, w, first, count):
-            above = [U[p, w, first, k] for k in range(K)]
-            here = [U[p, w, first + 1, k] for k in range(K)]
+            above = [U[p, w, first - 1, k] for k in range(K)]
+            here = [U[p, w, first, k] for k in range(K)]
             for i in range(count):
-                below = [U[p, w, first + 2 + i, k] for k in range(K)]
+                below = [U[p, w, first + 1 + i, k] for k in range(K)]
                 b = [4.0 * here[k] + (above[k] + below[k]) for k in range(K)]
                 line = [pltpu.roll(b[K - 1], 1, 0)] + b + [pltpu.roll(b[0], 7, 0)]
                 yield i, here, [(line[k] + line[k + 2]) + 4.0 * b[k] for k in range(K)]
                 above, here = here, below
 
-        def precondition(ge, w):
-            eig6, inv_centre, stretch, inv_spread = coefficients(w)
-            ic, ie = full(inv_centre), inv_eig[w]
-
-            def begin(i, c):
-                for e in (2 * i, 2 * i + 1):
+        def begin(ge, w, low, count):
+            ic, ie = full(coefficients(w)[1]), inv_eig[w]
+
+            def one(i, c):
+                for e in (low + 2 * i, low + 2 * i + 1):
                     for k in range(K):
                         g = ge[w, e, pl.ds(k, 8, stride=K), :]
                         G[w, e, k] = g * ie
                         u = g * ic
-                        U[0, w, e + 1, k] = u
+                        U[0, w, e, k] = u
                         DX[w, e, k] = u
                 return c
 
-            lax.fori_loop(0, ER // 2, begin, 0)
+            lax.fori_loop(0, count // 2, one, 0)
+
+        def sweeps(w, rows):
+            eig6, _, stretch, inv_spread = coefficients(w)
 
             def sweep(n, ratio):
                 p = n % 2
                 ratio_next = 1.0 / (2.0 * stretch - ratio)
                 momentum = full(ratio_next * ratio)
                 step = full(2.0 * ratio_next * inv_spread * eig6)
-                clipped = (ER - HALO + GROUP - 2 - n) // GROUP
-                groups = jnp.where(top | bottom, clipped, (ER + GROUP - 3 - 2 * n) // GROUP)
-                low = jnp.where(bottom, ER - HALO - GROUP * groups, ER // 2 - GROUP // 2 * groups)
-                low = jnp.where(top, HALO, low)
-
-                def group(i, c):
-                    first = low + GROUP * i
-                    for at, v, h in rows_of(p, w, first, GROUP):
+
+                def advance(first, count, edge):
+                    for at, v, h in rows_of(p, w, first, count):
                         e = first + at
+                        inside = 1
+                        if edge:
+                            above, below = top & (e < HALO), bottom & (e >= HALO + ROWS)
+                            inside = jnp.where(above | below, 0, 1)
                         for k in range(K):
                             dx = step * ((G[w, e, k] - SC[w, e, k] * v[k]) + h[k])
-                            dx = (momentum * DX[w, e, k] + dx) * MK[k]
+                            dx = (momentum * DX[w, e, k] + dx) * MK[inside, k]
                             DX[w, e, k] = dx
-                            U[1 - p, w, e + 1, k] = v[k] + dx
+                            U[1 - p, w, e, k] = v[k] + dx
+
+                rows(n, advance)
+                return ratio_next
+
+            lax.fori_loop(0, DEG - 1, sweep, 1.0 / stretch)
+
+        def inner(ge, n_halo, w):
+            halo_wait(ge, n_halo, w, SIDES)
+            begin(ge, w, HALO, ROWS)
+
+            def rows(n, advance):
+                def one(i, c):
+                    advance(HALO + 1 + n + 2 * i, 2, False)
                     return c
 
-                lax.fori_loop(0, groups, group, 0)
-                return ratio_next
-
-            lax.fori_loop(0, DEG - 1, sweep, 1.0 / stretch)
-
-        def stencil_part(w, keep):
+                lax.fori_loop(0, ROWS // 2 - 1 - n, one, 0)
+
+            sweeps(w, rows)
+
+        def outer(ge, n_halo, w):
+            halo_wait(ge, n_halo, w, ENDS)
+            begin(ge, w, 0, HALO)
+            begin(ge, w, HALO + ROWS, HALO)
+
+            def rows(n, advance):
+                def one(i, c):
+                    upper = n + 1 + GROUP * i
+                    lower = ROWS + HALO - 1 - n + GROUP * i - HALO
+                    advance(jnp.where(i < HALO // GROUP, upper, lower), GROUP, True)
+                    return c
+
+                lax.fori_loop(0, 2 * HALO // GROUP, one, 0)
+
+            sweeps(w, rows)
+
+        def keep_rows(w, keep):
+            def one(i, c):
+                for r in (2 * i, 2 * i + 1):
+                    for k in range(K):
+                        keep[w, r, pl.ds(k, 8, stride=K), :] = U[(DEG - 1) % 2, w, r + HALO, k]
+                return c
+
+            lax.fori_loop(0, ROWS // 2, one, 0)
+
+        def stencil_part(w):
             eig6 = full(coefficients(w)[0])
 
             def one(i, c):
@@ -446,7 +487,6 @@
                 for at, v, h in rows_of((DEG - 1) % 2, w, first + HALO, GROUP):
                     r = first + at
                     for k in range(K):
-                        keep[w, r, pl.ds(k, 8, stride=K), :] = v[k]
                         NQ[w, r, pl.ds(k, 8, stride=K), :] = eig6 * (KC[r + HALO, k] * v[k] - h[k])
                 return c
 
@@ -458,53 +498,38 @@
                 out = jnp.where(sub8 == at, jnp.sum(part, axis=0, keepdims=True), out)
             return out
 
-        def column_copy(at, i):
-            return pltpu.make_async_remote_copy(
-                src_ref=SA.at[at], dst_ref=RZ.at[at, z], send_sem=sum_send.at[at, 0],
-                recv_sem=sum_recv.at[at, 0],
-                device_id=(((z + i) & (Z - 1)) * Y + y, d), device_id_type=MESH,
-            )
-
-        def plane_copy(at, i):
-            return pltpu.make_async_remote_copy(
-                src_ref=SG.at[at], dst_ref=RG.at[at, j], send_sem=sum_send.at[at, 1],
-                recv_sem=sum_recv.at[at, 1],
-                device_id=device(z, ((j + i) & (J - 1))), device_id_type=MESH,
-            )
-
-        def wait_bytes(ref, count, sem):
-            part = ref.at[pl.ds(0, count)]
-            pltpu.make_async_copy(part, part, sem).wait()
-
-        def column_start(at, value):
-            SA[at] = value
-            RZ[at, z] = value
+        stages = (
+            (Z, z, lambda i: (((z + i) & (Z - 1)) * Y + y, d)),
+            (D, d, lambda i: (ri, (d + i) & (D - 1))),
+            (Y, y, lambda i: (z * Y + ((y + i) & (Y - 1)), d)),
+        )
+
+        def sum_start(at, stage, value):
+            count, me, target = stages[stage]
+            SA[at, stage] = value
+            RS[at, stage, me] = value
 
             def one(i, c):
-                column_copy(at, i).start()
+                pltpu.make_async_remote_copy(
+                    src_ref=SA.at[at, stage], dst_ref=RS.at[at, stage, me],
+                    send_sem=sum_send.at[at, stage], recv_sem=sum_recv.at[at, stage],
+                    device_id=target(i), device_id_type=MESH,
+                ).start()
                 return c
 
-            lax.fori_loop(1, Z, one, 0)
-
-        def column_end(at):
+            lax.fori_loop(1, count, one, 0)
+
+        def sum_end(at, stage):
+            count = stages[stage][0]
+            part = RS.at[at, stage, pl.ds(0, count - 1)]
             for side in (sum_recv, sum_send):
-                wait_bytes(RZ.at[at], Z - 1, side.at[at, 0])
-            return lax.fori_loop(1, Z, lambda i, c: c + RZ[at, i], RZ[at, 0])
-
-        def plane_start(at, value):
-            SG[at] = value
-            RG[at, j] = value
-
-            def one(i, c):
-                plane_copy(at, i).start()
-                return c
-
-            lax.fori_loop(1, J, one, 0)
-
-        def plane_end(at):
-            for side in (sum_recv, sum_send):
-                wait_bytes(RG.at[at], J - 1, side.at[at, 1])
-            total = lax.fori_loop(1, J, lambda i, c: c + RG[at, i], RG[at, 0])
+                pltpu.make_async_copy(part, part, side.at[at, stage]).wait()
+            total = RS[at, stage, 0]
+            for i in range(1, count):
+                total = total + RS[at, stage, i]
+            return total
+
+        def sum_values(total):
             return [jnp.sum(total[i : i + 1], axis=1, keepdims=True) for i in range(3)]
 
         zero = jnp.zeros((8, LANES), jnp.float32)
@@ -524,9 +549,11 @@
             halo_start(GE1, 0, w)
         send_tile(PS, XS, 1)
         for w in range(WIDE):
-            halo_wait(GE1, 0, w)
-            precondition(GE1, w)
-            stencil_part(w, NZ)
+            inner(GE1, 0, w)
+        for w in range(WIDE):
+            outer(GE1, 0, w)
+            keep_rows(w, NZ)
+            stencil_part(w)
         to_time(lambda w, rows: NZ[w, rows, OWN, :], TZ)
         all_wait(XS, 1)
         to_modes(lambda i: TZ[i] * XS[i], put_seen)
@@ -542,21 +569,25 @@
 
             sums = lax.fori_loop(0, ROWS, first_image, sums)
             halo_start(GE2, 1, w)
-        column_start(0, pack(sums))
+        sum_start(0, 0, pack(sums))
         send_days(TZ, FZ, 2)
         to_time(lambda w, rows: GE2[w, pl.ds(rows.start + HALO, rows.size), OWN, :], TQ)
         send_days(TQ, FQ, 3)
 
+        sum_start(0, 1, sum_end(0, 0))
         for w in range(WIDE):
-            halo_wait(GE2, 1, w)
-            precondition(GE2, w)
-            stencil_part(w, NW)
-            if w == 0:
-                plane_start(0, column_end(0))
+            inner(GE2, 1, w)
+        sum_start(0, 2, sum_end(0, 1))
+        for w in range(WIDE):
+            outer(GE2, 1, w)
+            keep_rows(w, NW)
+            if w + 1 < WIDE:
+                stencil_part(w)
         to_time(lambda w, rows: NW[w, rows, OWN, :], TW)
         send_days(TW, FW, 4)
+        stencil_part(WIDE - 1)
         to_modes(lambda i: TW[i] * XS[i], put_seen)
-        fit0, curve0, _ = plane_end(0)
+        fit0, curve0, _ = sum_values(sum_end(0, 2))
         alpha0 = fit0 / curve0
 
         sums = (zero, zero, zero)
@@ -574,13 +605,15 @@
                 )
 
             sums = lax.fori_loop(0, ROWS, second_image, sums)
-        column_start(1, pack(sums))
+        sum_start(1, 0, pack(sums))
         to_time(lambda w, rows: NV[w, rows], TV)
         own_days(TV, FV, 5)
-        send_range(to_days, TV, FV, 5, 1, 12)
-        plane_start(1, column_end(1))
-        send_range(to_days, TV, FV, 5, 12, J)
-        fit1, curve1, cross1 = plane_end(1)
+        send_range(to_days, TV, FV, 5, 1, 8)
+        sum_start(1, 1, sum_end(1, 0))
+        send_range(to_days, TV, FV, 5, 8, 20)
+        sum_start(1, 2, sum_end(1, 1))
+        send_range(to_days, TV, FV, 5, 20, J)
+        fit1, curve1, cross1 = sum_values(sum_end(1, 2))
         beta = fit1 / fit0
         alpha1 = fit1 / (curve1 + 2.0 * beta * cross1 + beta * beta * curve0)
         c_old = alpha0 + alpha1 + alpha1 * beta
@@ -597,7 +630,7 @@
                         values.append(PR[at] - c_old * FQ[at] + c_new * FV[at])
                 for r, v in enumerate(swap(values)):
                     for t in range(0, TB, 8):
-                        (sol, res)[part][day_rows(i, r, t), :] = v[t : t + 8]
+                        (sol_out, res_out)[part][day_rows(i, r, t), :] = v[t : t + 8]
                 return c
 
             lax.fori_loop(0, SLABS, one, 0)
@@ -605,9 +638,15 @@
         all_wait(FZ, 2)
         all_wait(FW, 4)
         finish(0)
+        outs = [
+            pltpu.make_async_copy(src, dst, out_sem.at[i])
+            for i, (src, dst) in enumerate(((sol_out, sol), (res_out, res)))
+        ]
+        outs[0].start()
         all_wait(FQ, 3)
         all_wait(FV, 5)
         finish(1)
+        outs[1].start()
 
         for at in range(6):
             all_wait_send(at)
@@ -619,6 +658,8 @@
         for n, ge in enumerate((GE1, GE2)):
             for w in range(WIDE):
                 each_way(3, lambda at: halo_copy(ge, n, w, at).wait_send())
+        for out in outs:
+            out.wait()
 
     f32 = jnp.float32
     extended = pltpu.VMEM((WIDE, ER, EC, LANES), f32)
@@ -633,16 +674,15 @@
     scratch = [
         given, pltpu.VMEM((TB * SLABS * RB, LANES), jnp.int32), pltpu.VMEM((RB, J * COLS), f32),
         pltpu.VMEM((RB, J * COLS), jnp.int32), pltpu.VMEM((NT, NT), f32), pltpu.VMEM((8, NT), f32),
-        extended, extended, pltpu.VMEM((2, WIDE, ER + 2, K, 8, LANES), f32),
+        extended, extended, pltpu.VMEM((2, WIDE, ER, K, 8, LANES), f32),
         fields, fields, cell, fields, pltpu.VMEM((2, ER, EC, LANES), f32),
-        pltpu.VMEM((K, 8, LANES), f32), flat, strip, strip, strip, flat, days, days, tile, tile,
+        pltpu.VMEM((2, K, 8, LANES), f32), flat, strip, strip, strip, flat, days, days, tile, tile,
         tile, tile, tile, tile, days, days, days, days,
         pltpu.VMEM((4, 8, LANES), f32), pltpu.VMEM((Y, 8, LANES), f32),
         pltpu.VMEM((8, LANES), f32), pltpu.VMEM((8, 8, LANES), f32),
-        pltpu.VMEM((2, 8, LANES), f32), pltpu.VMEM((2, Z, 8, LANES), f32),
-        pltpu.VMEM((2, 8, LANES), f32), pltpu.VMEM((2, J, 8, LANES), f32),
+        pltpu.VMEM((2, 3, 8, LANES), f32), pltpu.VMEM((2, 3, max(Z, D, Y), 8, LANES), f32), given, given,
         dma((2, WIDE, 8)), dma((2, WIDE, 8)), dma((8,)), dma((8,)), dma((6,)), dma((6,)),
-        dma((4,)), dma((Y,)), dma((2, 2)), dma((2, 2)), dma((6,)),
+        dma((4,)), dma((Y,)), dma((2, 3)), dma((2, 3)), dma((6,)), dma((2,)),
     ]
     return kernel, scratch
 
@@ -653,7 +693,6 @@
     kernel, scratch = make_kernel(Z, D)
     basis, modal = modal_constants(TB * D)
     slabs = Y * D // 4
-    vmem = pl.BlockSpec(memory_space=pltpu.VMEM)
     smem = pl.BlockSpec(memory_space=pltpu.SMEM)
     hbm = pl.BlockSpec(memory_space=pl.ANY)
 
@@ -671,7 +710,7 @@
             kernel,
             out_shape=(shape, shape),
             in_specs=[hbm] * 4 + [smem] + [hbm] * 2,
-            out_specs=(vmem, vmem),
+            out_specs=(hbm, hbm),
             scratch_shapes=scratch,
             compiler_params=pltpu.CompilerParams(
                 collective_id=0, has_side_effects=True, vmem_limit_bytes=56 * 1024 * 1024

time: 81.4 us -> 81.6 us (level)
  no operation moved by 1% of the time
where the time goes in v4:
time: 81.6 us; the launch traced here: 81.4 us
  Pallas kernels  78.1 us (96%)
  local copies, waits for them, and re-layouts  2.72 us (3%)
    pallas_call x1, Pallas kernels, body(): pl.pallas_call(kernel, out_shape=(shape, shape), in_specs=[hbm] * 4 + [sm...  78.1 us
    unnamed x4, local copies, waits for them, and re-layouts  2.72 us

profile of v4, /device:TPU:1, one launch (start us, length us, event | category | flops | bytes accessed | tf_op | source)
XLA Modules:
  0.0 81.4 jit_solution(2473107868527429772)
XLA Ops:
  0.6 78.1 %shard_map.86 = (f32[1024,128]{1,0:T(8,128)}, f32[1024,128]{1,0:T(8,128)}) custom-call(f32[1024,128]{1,0:T(8,128)} %bitcast.20, s32[1024,128]{1,0:T(8,128)} %bitcast.21, f32[4,1024]{1,0:T(4,128)} %weight_in.1, s32[4,1024]{1,0:T(4,128)} %classes_in.1, f32[16]{0:T(128)} %kappa.1, f32[256,256]{1,0:T(8,128)} %constant.4.clone.basis_in, ...), custom_call_target="tpu_custom_call" | custom-call | tf_op jit(solution)/shard_map/pallas_call | solution.py:709
  78.7 0.0 copy-start
  78.7 1.9 %copy.15 = f32[32,4,1024]{2,1,0:T(4,128)} copy(f32[32,4,1024]{2,1,0:T(4,128)} %bitcast.23) | data formatting | bytes 1048576
  80.6 0.0 copy-done
  80.6 0.8 copy.16
Async XLA Ops:
  78.7 1.9 %copy-start = (f32[1024,128]{1,0:T(8,128)S(1)}, f32[1024,128]{1,0:T(8,128)}, u32[]{:S(2)}) copy-start(f32[1024,128]{1,0:T(8,128)} %get-tuple-element.5) | copy-start | bytes 1572868

commit v5 on v4

--- a/solution.py
+++ b/solution.py
@@ -51,6 +51,7 @@
     J = Y * D
     WIDE = NT // LANES
     DBITS = D.bit_length() - 1
+    CBITS = (NT // COLS).bit_length() - 1
     SLABS = J // 4
     ER, EC = ROWS + 2 * HALO, COLS + 2 * HALO
     OWN = pl.ds(HALO, COLS)
@@ -58,8 +59,8 @@
     def kernel(
         obs_in, mask_in, weight_in, classes_in, kappa, basis_in, modal_in, sol, res,
         obs, mask, weight, classes, basis, modal,
-        GE1, GE2, U, DX, G, KC, SC, NC, MK, NAT, NQ, NZ, NW, NV, PR, PS, XR, XS,
-        TZ, TQ, TW, TV, FZ, FQ, FW, FV, PW, CW, CT, CN, SA, RS, sol_out, res_out,
+        GE1, GE2, U, DX, G, KC, SC, NC, MK, NAT, NQ, NZ, NW, PR, PS, XR, XS,
+        TZ, TQ, TW, TV, FZ, FQ, FW, FV, PW, CW, CT, CN, SA, RS, sol_out, res_out, RL, AZ, AQ, AW,
         halo_send, halo_recv, near_send, near_recv, all_send, all_recv, cell_send, cell_recv,
         sum_send, sum_recv, load_sem, out_sem,
     ):
@@ -158,6 +159,7 @@
             for r in range(RB):
                 seen = [obs[day_rows(i, r, t), :] for t in range(0, TB, 8)]
                 rhs.append(seen_rows(i, r) * jnp.concatenate(seen, axis=0))
+                RL[i, r] = rhs[r]
             for q, part in enumerate(swap(rhs)):
                 PR[4 * i + q] = part
             return c
@@ -375,12 +377,13 @@
 
             lax.fori_loop(0, Y // 2, one, 0)
 
-        def to_time(get, out):
+        def to_time(get, out, extra=None):
             def one(i, c):
                 v = [get(w, pl.ds(2 * RB * i, 2 * RB)).reshape(2 * RB * COLS, LANES) for w in range(WIDE)]
                 t = dot(basis[...], jnp.concatenate(v, axis=1), ((1,), (1,)))
-                out[2 * i] = t[:, :LANES]
-                out[2 * i + 1] = t[:, LANES:]
+                for half in range(2):
+                    part = t[:, half * LANES : (half + 1) * LANES]
+                    out[2 * i + half] = part if extra is None else part + extra(2 * i + half)
                 return c
 
             lax.fori_loop(0, Y // 2, one, 0)
@@ -499,9 +502,9 @@
             return out
 
         stages = (
-            (Z, z, lambda i: (((z + i) & (Z - 1)) * Y + y, d)),
             (D, d, lambda i: (ri, (d + i) & (D - 1))),
             (Y, y, lambda i: (z * Y + ((y + i) & (Y - 1)), d)),
+            (Z, z, lambda i: (((z + i) & (Z - 1)) * Y + y, d)),
         )
 
         def sum_start(at, stage, value):
@@ -574,6 +577,14 @@
         to_time(lambda w, rows: GE2[w, pl.ds(rows.start + HALO, rows.size), OWN, :], TQ)
         send_days(TQ, FQ, 3)
 
+        def swap_days(src, dst):
+            def one(i, c):
+                for r, v in enumerate(swap([src[4 * i + q] for q in range(4)])):
+                    dst[i, r] = v
+                return c
+
+            lax.fori_loop(0, SLABS, one, 0)
+
         sum_start(0, 1, sum_end(0, 0))
         for w in range(WIDE):
             inner(GE2, 1, w)
@@ -581,71 +592,75 @@
         for w in range(WIDE):
             outer(GE2, 1, w)
             keep_rows(w, NW)
+            if w == 0:
+                all_wait(FZ, 2)
+                swap_days(FZ, AZ)
             if w + 1 < WIDE:
                 stencil_part(w)
         to_time(lambda w, rows: NW[w, rows, OWN, :], TW)
-        send_days(TW, FW, 4)
         stencil_part(WIDE - 1)
-        to_modes(lambda i: TW[i] * XS[i], put_seen)
         fit0, curve0, _ = sum_values(sum_end(0, 2))
         alpha0 = fit0 / curve0
 
         sums = (zero, zero, zero)
         for w in range(WIDE):
             def second_image(r, acc):
-                fit, curve, cross = acc
+                fit, seen, cross = acc
                 wh, g = NW[w, r, OWN, :], GE2[w, r + HALO, OWN, :]
-                q = NQ[w, r, OWN, :] + NAT[w, r]
-                NV[w, r] = q
                 z1 = NZ[w, r, OWN, :] - alpha0 * wh
                 r1 = GE1[w, r + HALO, OWN, :] - alpha0 * g
                 return (
-                    fit + fold_cells(r1 * z1), curve + fold_cells(z1 * (g - alpha0 * q)),
+                    fit + fold_cells(r1 * z1), seen + fold_cells(z1 * NQ[w, r, OWN, :]),
                     cross + fold_cells(z1 * g),
                 )
 
             sums = lax.fori_loop(0, ROWS, second_image, sums)
-        sum_start(1, 0, pack(sums))
-        to_time(lambda w, rows: NV[w, rows], TV)
-        own_days(TV, FV, 5)
-        send_range(to_days, TV, FV, 5, 1, 8)
+
+        def seen_part(i, acc):
+            yt, t = i >> CBITS, pl.multiple_of((i & (NT // COLS - 1)) * COLS, COLS)
+            rows = pl.ds(t, COLS)
+            tw = TW[yt, rows]
+            return acc + fold_cells(XS[yt, rows] * (TZ[yt, rows] - alpha0 * tw) * tw)
+
+        fit, seen, cross = sums
+        seen = lax.fori_loop(0, Y * NT // COLS, seen_part, seen)
+        sum_start(1, 0, pack((fit, seen, cross)))
+        send_days(TW, FW, 4)
+        to_time(lambda w, rows: NQ[w, rows, OWN, :], TV, lambda i: XS[i] * TW[i])
         sum_start(1, 1, sum_end(1, 0))
-        send_range(to_days, TV, FV, 5, 8, 20)
+        send_days(TV, FV, 5)
         sum_start(1, 2, sum_end(1, 1))
-        send_range(to_days, TV, FV, 5, 20, J)
-        fit1, curve1, cross1 = sum_values(sum_end(1, 2))
+        all_wait(FQ, 3)
+        swap_days(FQ, AQ)
+        all_wait(FW, 4)
+        swap_days(FW, AW)
+        fit1, seen1, cross1 = sum_values(sum_end(1, 2))
+        curve1 = cross1 - alpha0 * seen1
         beta = fit1 / fit0
         alpha1 = fit1 / (curve1 + 2.0 * beta * cross1 + beta * beta * curve0)
         c_old = alpha0 + alpha1 + alpha1 * beta
         c_new = alpha0 * alpha1
 
-        def finish(part):
-            def one(i, c):
-                values = []
-                for q in range(4):
-                    at = 4 * i + q
-                    if part == 0:
-                        values.append(c_old * FZ[at] - c_new * FW[at])
-                    else:
-                        values.append(PR[at] - c_old * FQ[at] + c_new * FV[at])
-                for r, v in enumerate(swap(values)):
-                    for t in range(0, TB, 8):
-                        (sol_out, res_out)[part][day_rows(i, r, t), :] = v[t : t + 8]
-                return c
-
-            lax.fori_loop(0, SLABS, one, 0)
-
-        all_wait(FZ, 2)
-        all_wait(FW, 4)
-        finish(0)
+        def finish_solution(i, c):
+            lanes = pl.ds(pl.multiple_of(i * LANES, LANES), LANES)
+            for r in range(RB):
+                sol_out[r, :, lanes] = c_old * AZ[i, r] - c_new * AW[i, r]
+            return c
+
+        def finish_residual(i, c):
+            lanes = pl.ds(pl.multiple_of(i * LANES, LANES), LANES)
+            for r, v in enumerate(swap([FV[4 * i + q] for q in range(4)])):
+                res_out[r, :, lanes] = RL[i, r] - c_old * AQ[i, r] + c_new * v
+            return c
+
+        lax.fori_loop(0, SLABS, finish_solution, 0)
         outs = [
             pltpu.make_async_copy(src, dst, out_sem.at[i])
             for i, (src, dst) in enumerate(((sol_out, sol), (res_out, res)))
         ]
         outs[0].start()
-        all_wait(FQ, 3)
         all_wait(FV, 5)
-        finish(1)
+        lax.fori_loop(0, SLABS, finish_residual, 0)
         outs[1].start()
 
         for at in range(6):
@@ -670,17 +685,19 @@
     days = pltpu.VMEM((J, TB, LANES), f32)
     tile = pltpu.VMEM((Y, NT, LANES), f32)
     dma = pltpu.SemaphoreType.DMA
+    slab = pltpu.VMEM((SLABS, RB, TB, LANES), f32)
     given = pltpu.VMEM((TB * SLABS * RB, LANES), f32)
     scratch = [
         given, pltpu.VMEM((TB * SLABS * RB, LANES), jnp.int32), pltpu.VMEM((RB, J * COLS), f32),
         pltpu.VMEM((RB, J * COLS), jnp.int32), pltpu.VMEM((NT, NT), f32), pltpu.VMEM((8, NT), f32),
         extended, extended, pltpu.VMEM((2, WIDE, ER, K, 8, LANES), f32),
         fields, fields, cell, fields, pltpu.VMEM((2, ER, EC, LANES), f32),
-        pltpu.VMEM((2, K, 8, LANES), f32), flat, strip, strip, strip, flat, days, days, tile, tile,
+        pltpu.VMEM((2, K, 8, LANES), f32), flat, strip, strip, strip, days, days, tile, tile,
         tile, tile, tile, tile, days, days, days, days,
         pltpu.VMEM((4, 8, LANES), f32), pltpu.VMEM((Y, 8, LANES), f32),
         pltpu.VMEM((8, LANES), f32), pltpu.VMEM((8, 8, LANES), f32),
-        pltpu.VMEM((2, 3, 8, LANES), f32), pltpu.VMEM((2, 3, max(Z, D, Y), 8, LANES), f32), given, given,
+        pltpu.VMEM((2, 3, 8, LANES), f32), pltpu.VMEM((2, 3, max(Z, D, Y), 8, LANES), f32),
+        pltpu.VMEM((RB, TB, J * COLS), f32), pltpu.VMEM((RB, TB, J * COLS), f32), slab, slab, slab, slab,
         dma((2, WIDE, 8)), dma((2, WIDE, 8)), dma((8,)), dma((8,)), dma((6,)), dma((6,)),
         dma((4,)), dma((Y,)), dma((2, 3)), dma((2, 3)), dma((6,)), dma((2,)),
     ]
@@ -700,12 +717,8 @@
         array = array.reshape(TB, RB, slabs, LANES)
         return jnp.transpose(array, (0, 2, 1, 3)).reshape(TB * slabs * RB, LANES)
 
-    def by_row(array):
-        array = array.reshape(TB, slabs, RB, LANES)
-        return jnp.transpose(array, (0, 2, 1, 3)).reshape(TB, RB, slabs * LANES)
-
     def body(observations, obs_mask, obs_weight, classes, kappa_table):
-        shape = jax.ShapeDtypeStruct((TB * slabs * RB, LANES), jnp.float32)
+        shape = jax.ShapeDtypeStruct((RB, TB, slabs * LANES), jnp.float32)
         sol, res = pl.pallas_call(
             kernel,
             out_shape=(shape, shape),
@@ -719,7 +732,7 @@
             by_slab(observations), by_slab(obs_mask), obs_weight, classes, kappa_table,
             jnp.asarray(basis), jnp.asarray(modal),
         )
-        return by_row(sol), by_row(res)
+        return jnp.transpose(sol, (1, 0, 2)), jnp.transpose(res, (1, 0, 2))
 
     in_specs = (P("days", "rows", None), P("days", "rows", None), P("rows", None), P("rows", None), P())
     out_specs = (P("days", "rows", None), P("days", "rows", None))

time: 81.6 us -> 80.6 us (0.988)
  the two profiles are of different devices: /device:TPU:1 before, /device:TPU:2 now
where the time goes in v5:
time: 80.6 us; the launch traced here: 80.4 us
  Pallas kernels  76.4 us (95%)
  local copies, waits for them, and re-layouts  3.37 us (4%)
    pallas_call x1, Pallas kernels, body(): pl.pallas_call(kernel, out_shape=(shape, shape), in_specs=[hbm] * 4 + [sm...  76.4 us
    unnamed x4, local copies, waits for them, and re-layouts  3.37 us

profile of v5, /device:TPU:2, one launch (start us, length us, event | category | flops | bytes accessed | tf_op | source)
XLA Modules:
  0.0 80.4 jit_solution(16134763262090099394)
XLA Ops:
  0.6 76.4 %shard_map.86 = (f32[4,32,1024]{2,1,0:T(8,128)}, f32[4,32,1024]{2,1,0:T(8,128)}) custom-call(f32[1024,128]{1,0:T(8,128)} %bitcast.12, s32[1024,128]{1,0:T(8,128)} %bitcast.13, f32[4,1024]{1,0:T(4,128)} %weight_in.1, s32[4,1024]{1,0:T(4,128)} %classes_in.1, f32[16]{0:T(128)} %kappa.1, f32[256,256]{1,0:T(8,128)} %constant.4.clone.basis_in, ...), custom_call_target="tpu_custom_call" | custom-call | tf_op jit(solution)/shard_map/pallas_call | solution.py:722
  77.0 0.0 copy-start
  77.1 2.2 %copy.11 = f32[32,4,1024]{2,1,0:T(4,128)} copy(f32[32,4,1024]{2,0,1:T(8,128)} %bitcast.15) | data formatting | bytes 1048576
  79.3 0.0 copy-done
  79.3 1.1 %copy.12 = f32[32,4,1024]{2,1,0:T(4,128)} copy(f32[32,4,1024]{2,0,1:T(8,128)S(1)} %bitcast.14) | data formatting | bytes 1048576
Async XLA Ops:
  77.0 2.2 %copy-start = (f32[4,32,1024]{2,1,0:T(8,128)S(1)}, f32[4,32,1024]{2,1,0:T(8,128)}, u32[]{:S(2)}) copy-start(f32[4,32,1024]{2,1,0:T(8,128)} %get-tuple-element.5) | copy-start | bytes 1572868

commit v6 on v5

--- a/solution.py
+++ b/solution.py
@@ -561,6 +561,7 @@
         all_wait(XS, 1)
         to_modes(lambda i: TZ[i] * XS[i], put_seen)
 
+        send_days(TZ, FZ, 2)
         sums = (zero, zero)
         for w in range(WIDE):
             def first_image(r, acc):
@@ -573,7 +574,6 @@
             sums = lax.fori_loop(0, ROWS, first_image, sums)
             halo_start(GE2, 1, w)
         sum_start(0, 0, pack(sums))
-        send_days(TZ, FZ, 2)
         to_time(lambda w, rows: GE2[w, pl.ds(rows.start + HALO, rows.size), OWN, :], TQ)
         send_days(TQ, FQ, 3)
 

time: 80.6 us -> 85.1 us (1.056)
  Pallas kernels: 76.4 us -> 80.9 us
    pallas_call x1, Pallas kernels: 76.4 us -> 80.9 us  [body(): pl.pallas_call(kernel, out_shape=(shape, shape), in_specs=[hbm] * 4 + [sm...]
where the time goes in v6:
time: 85.1 us; the launch traced here: 84.9 us
  Pallas kernels  80.9 us (95%)
  local copies, waits for them, and re-layouts  3.37 us (4%)
    pallas_call x1, Pallas kernels, body(): pl.pallas_call(kernel, out_shape=(shape, shape), in_specs=[hbm] * 4 + [sm...  80.9 us
    unnamed x4, local copies, waits for them, and re-layouts  3.37 us

profile of v6, /device:TPU:2, one launch (start us, length us, event | category | flops | bytes accessed | tf_op | source)
XLA Modules:
  0.0 84.9 jit_solution(4801065456239902536)
XLA Ops:
  0.6 80.9 %shard_map.86 = (f32[4,32,1024]{2,1,0:T(8,128)}, f32[4,32,1024]{2,1,0:T(8,128)}) custom-call(f32[1024,128]{1,0:T(8,128)} %bitcast.12, s32[1024,128]{1,0:T(8,128)} %bitcast.13, f32[4,1024]{1,0:T(4,128)} %weight_in.1, s32[4,1024]{1,0:T(4,128)} %classes_in.1, f32[16]{0:T(128)} %kappa.1, f32[256,256]{1,0:T(8,128)} %constant.4.clone.basis_in, ...), custom_call_target="tpu_custom_call" | custom-call | tf_op jit(solution)/shard_map/pallas_call | solution.py:722
  81.6 0.0 copy-start
  81.6 2.2 %copy.11 = f32[32,4,1024]{2,1,0:T(4,128)} copy(f32[32,4,1024]{2,0,1:T(8,128)} %bitcast.15) | data formatting | bytes 1048576
  83.8 0.0 copy-done
  83.8 1.1 %copy.12 = f32[32,4,1024]{2,1,0:T(4,128)} copy(f32[32,4,1024]{2,0,1:T(8,128)S(1)} %bitcast.14) | data formatting | bytes 1048576
Async XLA Ops:
  81.6 2.2 %copy-start = (f32[4,32,1024]{2,1,0:T(8,128)S(1)}, f32[4,32,1024]{2,1,0:T(8,128)}, u32[]{:S(2)}) copy-start(f32[4,32,1024]{2,1,0:T(8,128)} %get-tuple-element.5) | copy-start | bytes 1572868
